TPU v7x, 32 devices: a whole 2x2x4 slice. The times are simulated.
32 devices in a mesh: scene: 4 (over y, x), blk: 8 (over z, core).
Axes of the slice: x: 2, y: 2, z: 4, core: 2. Of those that a mesh axis runs over, the one named last changes fastest.
Arguments:
- tokens_in: bfloat16 [8192, 1024], P(('scene', 'blk')), may hold values from -6 to 6
- view_heights: int32 [4, 4], P('scene'), may hold values from 8 to 24, as said below
- view_widths: int32 [4, 4], P('scene'), may hold values from 16 to 48
- view_scenes: int32 [4, 4], P('scene'), may hold values from 0 to 0, as said below
- out_grad: bfloat16 [8192, 1024], P(('scene', 'blk')), may hold values from -6 to 6
- w_qkv: bfloat16 [1024, 3072], P(('scene', 'blk')), may hold values from -0.1875 to 0.1875
- w_out: bfloat16 [1024, 1024], P(('scene', 'blk')), may hold values from -4 to 4
- w_up: bfloat16 [1024, 4096], P(('scene', 'blk')), may hold values from -0.1875 to 0.1875
- w_down: bfloat16 [4096, 1024], P(('scene', 'blk')), may hold values from -0.09375 to 0.09375
- norm1_gain: bfloat16 [1024], P(('scene', 'blk')), may hold values from 0.5 to 1.5
- norm1_bias: bfloat16 [1024], P(('scene', 'blk')), may hold values from -3 to 3
- norm2_gain: bfloat16 [1024], P(('scene', 'blk')), may hold values from 0.5 to 1.5
- norm2_bias: bfloat16 [1024], P(('scene', 'blk')), may hold values from -3 to 3
Outputs:
- layer_out: bfloat16 [8192, 1024], P(('scene', 'blk'))
- input_grad: float32 [8192, 1024], P(('scene', 'blk'))
- qkv_grad: float32 [1024, 3072], P(('scene', 'blk'))
- out_weight_grad: float32 [1024, 1024], P(('scene', 'blk'))
- up_grad: float32 [1024, 4096], P(('scene', 'blk'))
- down_grad: float32 [4096, 1024], P(('scene', 'blk'))
- gain1_grad: float32 [1024], P(('scene', 'blk'))
- bias1_grad: float32 [1024], P(('scene', 'blk'))
- gain2_grad: float32 [1024], P(('scene', 'blk'))
- bias2_grad: float32 [1024], P(('scene', 'blk'))
Inputs may be any that keep to these rules, and one draw needn't show every extreme that they name: `view_heights`: within each group the views can be taken in fours whose areas add up to 2048; so a group's areas add up to 2048. `view_scenes`: each scene number of a group names exactly four of its views; the first and the last view of a group belong to one scene.
All inputs are finite; a program needn't handle non-finite values.
Results may differ from a plain program's by a relative error of at most 0.014.
Values may be sent and summed in bfloat16 or wider, within the bound.
No kernel may reach another device: no remote copies, remote signals or barrier semaphores. Data moves between devices by JAX's collectives and lax.ppermute only.
A program may use at most 256 MiB of HBM per device.

v0:
```python
import math

import jax
import jax.numpy as jnp
from jax import lax
from jax.sharding import PartitionSpec as P

D = 1024
HEADS = 16
HEAD_DIM = 64


EPSILON = 1e-05
MASKED = -1e30


def layer_norm(values, gain_row, bias_row):
    centred = values - jnp.mean(values, axis=1, keepdims=True)
    scaled = centred * lax.rsqrt(jnp.mean(centred * centred, axis=1, keepdims=True) + EPSILON)
    return scaled * gain_row + bias_row


def scene_rows(view_ends, labels, first_row, count_rows):
    places = first_row + jnp.arange(count_rows, dtype=jnp.int32)
    view_index = jnp.sum((places[:, None] >= view_ends[None, :]).astype(jnp.int32), axis=1)
    matches = view_index[:, None] == jnp.arange(labels.shape[0], dtype=jnp.int32)[None, :]
    return jnp.sum(jnp.where(matches, labels[None, :], 0), axis=1)


def in_blocks(update, carry, members):
    total_rows = members[0].shape[0]
    width_rows = math.gcd(total_rows, 1024)
    block_count = total_rows // width_rows
    stacked = tuple(
        (member.reshape((block_count, width_rows) + member.shape[1:]) for member in members)
    )

    def advance(state_now, indexed):
        block_index, block_parts = indexed
        return (update(state_now, block_parts, block_index * width_rows), None)

    carry, _ = lax.scan(advance, carry, (jnp.arange(block_count, dtype=jnp.int32), stacked))
    return carry


def heads_of(rows):
    return rows.reshape(rows.shape[0], HEADS, HEAD_DIM)


def pair_terms(
    query_heads, delta_heads, log_rows, probe_rows, allowed, key_heads, value_heads, score_scale
):
    raw = (
        jnp.einsum("qhe,khe->hqk", query_heads, key_heads, preferred_element_type=jnp.float32)
        * score_scale
    )
    weights_now = jnp.where(allowed, jnp.exp(raw - log_rows[:, :, None]), 0.0)
    backward = jnp.einsum(
        "qhe,khe->hqk", delta_heads, value_heads, preferred_element_type=jnp.float32
    )
    score_delta = (weights_now * (backward - probe_rows[:, :, None])).astype(jnp.bfloat16)
    return (weights_now.astype(jnp.bfloat16), score_delta)


def outer(left, right):
    return lax.dot_general(
        left, right, (((0,), (0,)), ((), ())), preferred_element_type=jnp.float32
    )


def against(left, right):
    return lax.dot_general(
        left, right, (((1,), (1,)), ((), ())), preferred_element_type=jnp.float32
    )


def on_device(
    tokens_in,
    view_heights,
    view_widths,
    view_scenes,
    out_grad,
    w_qkv,
    w_out,
    w_up,
    w_down,
    norm1_gain,
    norm1_bias,
    norm2_gain,
    norm2_bias,
):
    gathered = (
        lax.all_gather(w_qkv, ("scene", "blk"), axis=0, tiled=True),
        lax.all_gather(w_out, ("scene", "blk"), axis=0, tiled=True),
        lax.all_gather(w_up, ("scene", "blk"), axis=0, tiled=True),
        lax.all_gather(w_down, ("scene", "blk"), axis=0, tiled=True),
        lax.all_gather(norm1_gain, ("scene", "blk"), axis=0, tiled=True),
        lax.all_gather(norm1_bias, ("scene", "blk"), axis=0, tiled=True),
        lax.all_gather(norm2_gain, ("scene", "blk"), axis=0, tiled=True),
        lax.all_gather(norm2_bias, ("scene", "blk"), axis=0, tiled=True),
    )
    full_qkv, full_out, full_up, full_down = (gathered[0], gathered[1], gathered[2], gathered[3])
    gain_one = gathered[4].astype(jnp.float32)
    bias_one = gathered[5].astype(jnp.float32)
    gain_two = gathered[6].astype(jnp.float32)
    bias_two = gathered[7].astype(jnp.float32)
    local_rows = tokens_in.shape[0]
    view_ends = jnp.cumsum(view_heights[0] * view_widths[0])
    labels = view_scenes[0]
    own_first = lax.axis_index("blk") * local_rows
    own_scene = scene_rows(view_ends, labels, own_first, local_rows)
    score_scale = HEAD_DIM ** (-0.5)
    inputs = tokens_in.astype(jnp.float32)
    normed, norm_one_pull = jax.vjp(layer_norm, inputs, gain_one, bias_one)
    normed_low = normed.astype(jnp.bfloat16)
    projected = jnp.dot(normed_low, full_qkv, preferred_element_type=jnp.float32).astype(
        jnp.bfloat16
    )
    query_rows = projected[:, :D]
    key_rows = projected[:, D : 2 * D]
    value_rows = projected[:, 2 * D :]
    query_heads = heads_of(query_rows)

    def forward_update(state_now, members, first_row):
        run_max, run_sum, run_total = state_now
        piece_keys, piece_values = members
        piece_rows = piece_keys.shape[0]
        key_scene = scene_rows(view_ends, labels, first_row, piece_rows)
        allowed = (own_scene[:, None] == key_scene[None, :])[None]
        raw = (
            jnp.einsum(
                "qhe,khe->hqk",
                query_heads,
                heads_of(piece_keys),
                preferred_element_type=jnp.float32,
            )
            * score_scale
        )
        new_max = jnp.maximum(run_max, jnp.max(jnp.where(allowed, raw, MASKED), axis=2))
        expo = jnp.where(allowed, jnp.exp(raw - new_max[:, :, None]), 0.0)
        factor = jnp.exp(run_max - new_max)
        run_sum = run_sum * factor + jnp.sum(expo, axis=2)
        mixed = jnp.einsum(
            "hqk,khe->qhe",
            expo.astype(jnp.bfloat16),
            heads_of(piece_values),
            preferred_element_type=jnp.float32,
        )
        run_total = run_total * jnp.transpose(factor)[:, :, None] + mixed
        return (new_max, run_sum, run_total)

    start_state = (
        jnp.full((HEADS, local_rows), MASKED, jnp.float32),
        jnp.zeros((HEADS, local_rows), jnp.float32),
        jnp.zeros((local_rows, HEADS, HEAD_DIM), jnp.float32),
    )
    run_max, run_sum, run_total = in_blocks(
        forward_update,
        start_state,
        (
            lax.all_gather(key_rows, "blk", axis=0, tiled=True),
            lax.all_gather(value_rows, "blk", axis=0, tiled=True),
        ),
    )
    log_total = run_max + jnp.log(run_sum)
    attended_heads = run_total / jnp.transpose(run_sum)[:, :, None]
    attended_low = attended_heads.reshape(local_rows, D).astype(jnp.bfloat16)
    hidden = inputs + jnp.dot(attended_low, full_out, preferred_element_type=jnp.float32)
    normed_two, norm_two_pull = jax.vjp(layer_norm, hidden, gain_two, bias_two)
    normed_two_low = normed_two.astype(jnp.bfloat16)
    upward = jnp.dot(normed_two_low, full_up, preferred_element_type=jnp.float32)
    active, gelu_pull = jax.vjp(jax.nn.gelu, upward)
    active_low = active.astype(jnp.bfloat16)
    result = (hidden + jnp.dot(active_low, full_down, preferred_element_type=jnp.float32)).astype(
        jnp.bfloat16
    )
    down_term = outer(active_low, out_grad)
    up_delta = gelu_pull(against(out_grad, full_down))[0].astype(jnp.bfloat16)
    up_term = outer(normed_two_low, up_delta)
    hidden_back, gain_two_term, bias_two_term = norm_two_pull(against(up_delta, full_up))
    hidden_delta = out_grad.astype(jnp.float32) + hidden_back
    hidden_low = hidden_delta.astype(jnp.bfloat16)
    out_term = outer(attended_low, hidden_low)
    att_delta = against(hidden_low, full_out).astype(jnp.bfloat16)
    delta_heads = heads_of(att_delta)
    row_probe = jnp.transpose(jnp.sum(delta_heads.astype(jnp.float32) * attended_heads, axis=2))
    query_start = jnp.zeros((local_rows, HEADS, HEAD_DIM), jnp.float32)
    every_key, every_value = (
        lax.all_gather(key_rows, "blk", axis=0, tiled=True),
        lax.all_gather(value_rows, "blk", axis=0, tiled=True),
    )
    group_rows = every_key.shape[0]
    width_rows = math.gcd(group_rows, 1024)
    block_count = group_rows // width_rows

    def joint_step(total, indexed):
        block_index, block_keys, block_values = indexed
        block_first = block_index * width_rows
        key_heads = heads_of(block_keys)
        value_heads = heads_of(block_values)
        key_scene = scene_rows(view_ends, labels, block_first, width_rows)
        allowed = (own_scene[:, None] == key_scene[None, :])[None]
        weights_low, score_delta = pair_terms(
            query_heads,
            delta_heads,
            log_total,
            row_probe,
            allowed,
            key_heads,
            value_heads,
            score_scale,
        )
        total = (
            total
            + jnp.einsum("hqk,khe->qhe", score_delta, key_heads, preferred_element_type=jnp.float32)
            * score_scale
        )
        value_part = jnp.einsum(
            "hqk,qhe->khe", weights_low, delta_heads, preferred_element_type=jnp.float32
        )
        key_part = (
            jnp.einsum("hqk,qhe->khe", score_delta, query_heads, preferred_element_type=jnp.float32)
            * score_scale
        )
        rows_out = jnp.concatenate(
            [key_part.reshape(width_rows, D), value_part.reshape(width_rows, D)], axis=1
        )
        return (total, rows_out)

    query_total, pair_rows = lax.scan(
        joint_step,
        query_start,
        (
            jnp.arange(block_count, dtype=jnp.int32),
            every_key.reshape(block_count, width_rows, D),
            every_value.reshape(block_count, width_rows, D),
        ),
    )
    pair_rows = pair_rows.reshape(group_rows, 2 * D)
    both_sums = lax.psum_scatter(
        pair_rows.astype(jnp.bfloat16), "blk", scatter_dimension=0, tiled=True
    ).astype(jnp.float32)
    key_total = both_sums[:, :D]
    value_total = both_sums[:, D:]
    qkv_delta = jnp.concatenate(
        [query_total.reshape(local_rows, D), key_total, value_total], axis=1
    ).astype(jnp.bfloat16)
    qkv_term = outer(normed_low, qkv_delta)
    input_back, gain_one_term, bias_one_term = norm_one_pull(against(qkv_delta, full_qkv))
    input_grad = hidden_delta + input_back
    summed = (
        lax.psum_scatter(qkv_term, ("scene", "blk"), scatter_dimension=0, tiled=True),
        lax.psum_scatter(out_term, ("scene", "blk"), scatter_dimension=0, tiled=True),
        lax.psum_scatter(up_term, ("scene", "blk"), scatter_dimension=0, tiled=True),
        lax.psum_scatter(down_term, ("scene", "blk"), scatter_dimension=0, tiled=True),
        lax.psum_scatter(gain_one_term, ("scene", "blk"), scatter_dimension=0, tiled=True),
        lax.psum_scatter(bias_one_term, ("scene", "blk"), scatter_dimension=0, tiled=True),
        lax.psum_scatter(gain_two_term, ("scene", "blk"), scatter_dimension=0, tiled=True),
        lax.psum_scatter(bias_two_term, ("scene", "blk"), scatter_dimension=0, tiled=True),
    )
    return (
        result,
        input_grad,
        summed[0],
        summed[1],
        summed[2],
        summed[3],
        summed[4],
        summed[5],
        summed[6],
        summed[7],
    )


def solution(mesh):
    in_specs = (
        P(("scene", "blk"), None),
        P("scene", None),
        P("scene", None),
        P("scene", None),
        P(("scene", "blk"), None),
        P(("scene", "blk"), None),
        P(("scene", "blk"), None),
        P(("scene", "blk"), None),
        P(("scene", "blk"), None),
        P(("scene", "blk")),
        P(("scene", "blk")),
        P(("scene", "blk")),
        P(("scene", "blk")),
    )
    out_specs = (
        P(("scene", "blk"), None),
        P(("scene", "blk"), None),
        P(("scene", "blk"), None),
        P(("scene", "blk"), None),
        P(("scene", "blk"), None),
        P(("scene", "blk"), None),
        P(("scene", "blk")),
        P(("scene", "blk")),
        P(("scene", "blk")),
        P(("scene", "blk")),
    )
    return jax.shard_map(
        on_device, mesh=mesh, in_specs=in_specs, out_specs=out_specs, check_vma=False
    )
```

profile of v0, /device:TPU:0, one launch (start us, length us, event | category | flops | bytes accessed | tf_op | source)
XLA Modules:
  0.0 1305.1 jit_solution(17321014293332909345)
XLA Ops:
  12.1 42.5 %all-reduce.9 = (bf16[1024]{0:T(1024)(128)(2,1)S(1)}, bf16[1024]{0:T(1024)(128)(2,1)S(1)}, bf16[1024]{0:T(1024)(128)(2,1)S(1)}, bf16[1024]{0:T(1024)(128)(2,1)S(1)}) all-reduce(bf16[1024]{0:T(1024)(128)(2,1)S(1)} %dynamic-update-slice.1, bf16[1024]{0:T(1024)(128)(2,1)S(1)} %dynamic-update-slice, ...), channel_id=1, replica_groups=mesh['scene'=4,'blk'=8] {'scene','blk'}, use_global_device_ids=true, to_apply=%add.1 | all-reduce | flops 4096 | bytes 16384
  57.7 25.7 %all-gather.7.cloned.1.call-done = bf16[1024,3072]{1,0:T(8,128)(2,1)} async-done(((bf16[32,3072]{1,0:T(8,128)(2,1)}), bf16[1024,3072]{1,0:T(8,128)(2,1)}) %all-gather.7.cloned.1.call-update) | async-done | bytes 6291472 | tf_op jit(solution)/shard_map/all_gather | solution.py:93
  83.5 4.9 convolution_convert_fusion
  92.0 70.4 %all-gather.17.cloned.1.call-done = bf16[4096,1024]{1,0:T(8,128)(2,1)} async-done(((bf16[128,1024]{1,0:T(8,128)(2,1)}), bf16[4096,1024]{1,0:T(8,128)(2,1)}) %all-gather.17.cloned.1.call-update) | async-done | bytes 8388624 | tf_op jit(solution)/shard_map/all_gather | solution.py:96
  162.4 7.7 fusion.65
  170.1 40.2 %all-gather.9.cloned.1.call-done = bf16[2048,1024]{1,0:T(8,128)(2,1)} async-done(((bf16[256,1024]{1,0:T(8,128)(2,1)}), bf16[2048,1024]{1,0:T(8,128)(2,1)}) %all-gather.9.cloned.1.call-update) | async-done | bytes 4194320 | tf_op jit(solution)/shard_map/all_gather | solution.py:161
  210.3 17.2 %copy.77 = bf16[2,1024,1024]{1,2,0:T(8,128)(2,1)} copy(bf16[2,1024,1024]{2,1,0:T(8,128)(2,1)} %bitcast.172) | data formatting | bytes 8388608
  227.6 30.7 %all-gather.11.cloned.1.call-done = bf16[2048,1024]{1,0:T(8,128)(2,1)} async-done(((bf16[256,1024]{1,0:T(8,128)(2,1)}), bf16[2048,1024]{1,0:T(8,128)(2,1)}) %all-gather.11.cloned.1.call-update) | async-done | bytes 4194320 | tf_op jit(solution)/shard_map/all_gather | solution.py:162
  258.2 6.3 copy.78
  264.5 60.9 %while.28 = (s32[]{:T(128)}, f32[16,256]{1,0:T(8,128)S(1)}, f32[16,256]{1,0:T(8,128)S(1)}, f32[256,16,64]{0,2,1:T(8,128)S(1)}, s32[256]{0:T(256)S(1)}, /*index=5...) while((s32[]{:T(128)}, f32[16,256]{1,0:T(8,128)S(1)}, ...), condition=%wide.region_10.11_spmd.clone, body=%wide.region_5.10_spmd.clone.sunk | while | flops 1120975872 | bytes 66872532 | solution.py:42
  266.2 4.0 constant_dynamic-slice_fusion.6
  270.2 7.3 fusion.122
  277.5 9.1 fusion.124
  286.6 8.3 fusion.126
  296.6 4.0 constant_dynamic-slice_fusion.6
  300.6 7.3 fusion.122
  307.9 9.2 fusion.124
  317.2 8.2 fusion.126
  329.2 66.3 %all-gather.15.cloned.1.call-done = bf16[1024,4096]{1,0:T(8,128)(2,1)} async-done(((bf16[32,4096]{1,0:T(8,128)(2,1)}), bf16[1024,4096]{1,0:T(8,128)(2,1)}) %all-gather.15.cloned.1.call-update) | async-done | bytes 8388624 | tf_op jit(solution)/shard_map/all_gather | solution.py:95
  395.4 11.2 fusion.33
  408.0 3.2 multiply_reduce_fusion
  416.2 116.7 %while.29 = (s32[]{:T(128)}, f32[256,16,64]{0,2,1:T(8,128)}, bf16[2,1024,2048]{2,1,0:T(8,128)(2,1)}, bf16[2,1024,1024]{1,2,0:T(8,128)(2,1)}, s32[256]{0:T(256)S(...) while((s32[]{:T(128)}, f32[256,16,64]{0,2,1:T(8,128)}, ...), condition=%wide.region_19.20_spmd.clone, body=%wide.region_16.19_spmd.clone.sunk | while | flops 2737855488 | bytes 124593384 | solution.py:230
  419.3 8.1 fusion.137
  429.0 10.7 fusion.138
  439.7 5.9 fusion.139
  445.6 9.1 fusion.140
  454.7 6.0 convolution_multiply_fusion.3
  463.2 6.5 copy.104
  469.7 4.8 constant_dynamic-update-slice_fusion.2
  477.2 8.1 fusion.137
  487.0 10.7 fusion.138
  497.7 6.1 fusion.139
  503.8 9.1 fusion.140
  512.9 6.0 convolution_multiply_fusion.3
  521.5 6.5 copy.104
  527.9 4.7 constant_dynamic-update-slice_fusion.2
  534.0 2.8 fusion.66
  538.4 9.9 fusion.57
  549.3 10.8 fusion.59
  563.4 57.8 %reduce-scatter.6.cloned.1.call-done = bf16[256,2048]{1,0:T(8,128)(2,1)} async-done(((bf16[2048,2048]{1,0:T(8,128)(2,1)}), bf16[256,2048]{1,0:T(8,128)(2,1)}) %reduce-scatter.6.cloned.1.call-update) | async-done | bytes 1048592 | tf_op jit(solution)/shard_map/reduce_scatter | solution.py:240
  621.3 7.7 fusion.46
  629.0 8.3 fusion.38
  637.3 5.0 fusion.60
  642.9 38.4 %all-reduce.8 = (f32[1024]{0:T(1024)S(1)}, f32[1024]{0:T(1024)S(1)}, f32[1024]{0:T(1024)S(1)}, f32[1024]{0:T(1024)S(1)}) all-reduce(f32[1024]{0:T(1024)S(1)} %get-tuple-element.342, f32[1024]{0:T(1024)S(1)} %get-tuple-element.345, f32[1024]{0:T(1024)S(1)} %copy-done.42, ...), channel_id=7, replica_groups=mesh['scene'=4,'blk'=8] {'scene','blk'}, use_global_device_ids=true, to_apply=%region_28.29.clone | all-reduce | flops 4096 | bytes 32768
  685.2 79.7 %reduce-scatter.10.cloned.1.call-done = f32[32,1024]{1,0:T(8,128)} async-done(((f32[1024,1024]{1,0:T(8,128)}), f32[32,1024]{1,0:T(8,128)}) %reduce-scatter.10.cloned.1.call-update) | async-done | bytes 131088 | tf_op jit(solution)/shard_map/reduce_scatter | solution.py:253
  764.8 186.7 %reduce-scatter.12.cloned.1.call-done = f32[32,4096]{1,0:T(8,128)} async-done(((f32[1024,4096]{1,0:T(8,128)}), f32[32,4096]{1,0:T(8,128)}) %reduce-scatter.12.cloned.1.call-update) | async-done | bytes 524304 | tf_op jit(solution)/shard_map/reduce_scatter | solution.py:254
  951.5 187.2 %reduce-scatter.14.cloned.1.call-done = f32[128,1024]{1,0:T(8,128)} async-done(((f32[4096,1024]{1,0:T(8,128)}), f32[128,1024]{1,0:T(8,128)}) %reduce-scatter.14.cloned.1.call-update) | async-done | bytes 524304 | tf_op jit(solution)/shard_map/reduce_scatter | solution.py:255
  1138.7 159.7 %reduce-scatter.8.cloned.1.call-done = f32[32,3072]{1,0:T(8,128)} async-done(((f32[1024,3072]{1,0:T(8,128)}), f32[32,3072]{1,0:T(8,128)}) %reduce-scatter.8.cloned.1.call-update) | async-done | bytes 393232 | tf_op jit(solution)/shard_map/reduce_scatter | solution.py:252
  (200 shorter events, 47.1 us)
Async XLA Ops:
  7.2 76.3 %all-gather.7.cloned.1.call-start = ((), (), s32[]{:S(2)}) async-start(), calls=%async_computation.5 | async-start | bytes 6488064 | tf_op jit(solution)/shard_map/all_gather | solution.py:93
  7.9 154.5 %all-gather.17.cloned.1.call-start = ((), (), s32[]{:S(2)}) async-start(), calls=%async_computation.10 | async-start | bytes 8650752 | tf_op jit(solution)/shard_map/all_gather | solution.py:96
  8.7 201.7 %all-gather.9.cloned.1.call-start = ((), (), s32[]{:S(2)}) async-start(), calls=%async_computation.6 | async-start | bytes 4718592 | tf_op jit(solution)/shard_map/all_gather | solution.py:161
  54.6 28.9 %copy-start.25 = (f32[1024]{0:T(1024)}, f32[1024]{0:T(1024)S(1)}, u32[]{:S(2)}) copy-start(f32[1024]{0:T(1024)S(1)} %convert_element_type.80) | copy-start | bytes 12292
  54.6 28.9 %copy-start.21 = (f32[1024]{0:T(1024)}, f32[1024]{0:T(1024)S(1)}, u32[]{:S(2)}) copy-start(f32[1024]{0:T(1024)S(1)} %convert_element_type.79) | copy-start | bytes 12292
  55.8 27.7 %copy-start.30 = (f32[256]{0:T(256)}, f32[256]{0:T(256)S(1)}, u32[]{:S(2)}) copy-start(f32[256]{0:T(256)S(1)} %broadcast_multiply_fusion.1) | copy-start | bytes 3076
  57.7 25.7 %copy-start.32 = (f32[256]{0:T(256)}, f32[256]{0:T(256)S(1)}, u32[]{:S(2)}) copy-start(f32[256]{0:T(256)S(1)} %fusion.50) | copy-start | bytes 3076
  88.4 3.0 copy-start.45
  88.4 3.0 copy-start.46
  88.4 3.3 copy-start.29
  88.4 74.0 %copy-start.9 = (bf16[256,1024]{1,0:T(8,128)(2,1)S(1)}, bf16[256,1024]{1,0:T(8,128)(2,1)}, u32[]{:S(2)}) copy-start(bf16[256,1024]{1,0:T(8,128)(2,1)} %param.21) | copy-start | bytes 1572868
  89.5 168.7 %all-gather.11.cloned.1.call-start = ((), (), s32[]{:S(2)}) async-start(), calls=%async_computation.7 | async-start | bytes 4718592 | tf_op jit(solution)/shard_map/all_gather | solution.py:162
  90.1 235.5 %all-gather.13.cloned.1.call-start = ((), (), s32[]{:S(2)}) async-start(), calls=%async_computation.8 | async-start | bytes 2162688 | tf_op jit(solution)/shard_map/all_gather | solution.py:94
  90.7 304.7 %all-gather.15.cloned.1.call-start = ((), (), s32[]{:S(2)}) async-start(), calls=%async_computation.9 | async-start | bytes 8650752 | tf_op jit(solution)/shard_map/all_gather | solution.py:95
  91.3 530.0 %reduce-scatter.6.cloned.1.call-start = ((), (), s32[]{:S(2)}) async-start(), calls=%async_computation.11 | async-start | bytes 9437184 | tf_op jit(solution)/shard_map/reduce_scatter | solution.py:240
  91.6 303.8 %copy-start.27 = (f32[1024]{0:T(1024)}, f32[1024]{0:T(1024)S(1)}, u32[]{:S(2)}) copy-start(f32[1024]{0:T(1024)S(1)} %convert_element_type.86) | copy-start | bytes 12292
  91.6 319.6 %copy-start.23 = (f32[1024]{0:T(1024)}, f32[1024]{0:T(1024)S(1)}, u32[]{:S(2)}) copy-start(f32[1024]{0:T(1024)S(1)} %convert_element_type.85) | copy-start | bytes 12292
  264.5 61.9 %copy-start.1 = (bf16[256,1024]{1,0:T(8,128)(2,1)S(1)}, bf16[256,1024]{1,0:T(8,128)(2,1)}, u32[]{:S(2)}) copy-start(bf16[256,1024]{1,0:T(8,128)(2,1)} %param.17) | copy-start | bytes 1572868
  325.6 81.1 %copy-start.7 = (bf16[256,16,64]{0,2,1:T(8,128)(2,1)}, bf16[256,16,64]{0,2,1:T(8,128)(2,1)S(1)}, u32[]{:S(2)}) copy-start(bf16[256,16,64]{0,2,1:T(8,128)(2,1)S(1)} %fusion.49) | copy-start | bytes 1572868
  328.9 82.4 %copy-start.3 = (f32[256,1024]{1,0:T(8,128)}, f32[256,1024]{1,0:T(8,128)S(1)}, u32[]{:S(2)}) copy-start(f32[256,1024]{1,0:T(8,128)S(1)} %get-tuple-element.417) | copy-start | bytes 3145732
  328.9 82.4 %copy-start.34 = (f32[256]{0:T(256)}, f32[256]{0:T(256)S(1)}, u32[]{:S(2)}) copy-start(f32[256]{0:T(256)S(1)} %broadcast_multiply_fusion) | copy-start | bytes 3076
  329.2 82.1 %copy-start.36 = (f32[256]{0:T(256)}, f32[256]{0:T(256)S(1)}, u32[]{:S(2)}) copy-start(f32[256]{0:T(256)S(1)} %fusion.51) | copy-start | bytes 3076
  395.4 12.6 copy-start.44
  408.0 4.6 copy-start.10
  411.2 2.0 copy-start.14
  411.7 4.3 copy-start.13
  411.7 3.0 copy-start.38
  413.2 3.0 copy-start.17
  532.9 231.9 %reduce-scatter.10.cloned.1.call-start = ((), (), s32[]{:S(2)}) async-start(), calls=%async_computation.13 | async-start | bytes 4325376 | tf_op jit(solution)/shard_map/reduce_scatter | solution.py:253
  536.8 1.5 copy-start.24
  536.8 1.5 copy-start.28
  536.8 1.5 copy-start.35
  536.9 414.7 %reduce-scatter.12.cloned.1.call-start = ((), (), s32[]{:S(2)}) async-start(), calls=%async_computation.14 | async-start | bytes 17301504 | tf_op jit(solution)/shard_map/reduce_scatter | solution.py:254
  548.3 590.4 %reduce-scatter.14.cloned.1.call-start = ((), (), s32[]{:S(2)}) async-start(), calls=%async_computation.15 | async-start | bytes 17301504 | tf_op jit(solution)/shard_map/reduce_scatter | solution.py:255
  560.1 61.2 %copy-start.2 = (bf16[256,1024]{1,0:T(8,128)(2,1)S(1)}, bf16[256,1024]{1,0:T(8,128)(2,1)}, u32[]{:S(2)}) copy-start(bf16[256,1024]{1,0:T(8,128)(2,1)} %param.17) | copy-start | bytes 1572868
  560.1 61.2 %copy-start.22 = (f32[1024]{0:T(1024)S(1)}, f32[1024]{0:T(1024)}, u32[]{:S(2)}) copy-start(f32[1024]{0:T(1024)} %copy-done.21) | copy-start | bytes 12292
  560.1 61.2 %copy-start.26 = (f32[1024]{0:T(1024)S(1)}, f32[1024]{0:T(1024)}, u32[]{:S(2)}) copy-start(f32[1024]{0:T(1024)} %copy-done.25) | copy-start | bytes 12292
  560.1 61.2 %copy-start.31 = (f32[256]{0:T(256)S(1)}, f32[256]{0:T(256)}, u32[]{:S(2)}) copy-start(f32[256]{0:T(256)} %copy-done.30) | copy-start | bytes 3076
  560.1 61.2 %copy-start.33 = (f32[256]{0:T(256)S(1)}, f32[256]{0:T(256)}, u32[]{:S(2)}) copy-start(f32[256]{0:T(256)} %copy-done.32) | copy-start | bytes 3076
  560.1 738.3 %reduce-scatter.8.cloned.1.call-start = ((), (), s32[]{:S(2)}) async-start(), calls=%async_computation.12 | async-start | bytes 12976128 | tf_op jit(solution)/shard_map/reduce_scatter | solution.py:252
  563.4 65.5 %copy-start.15 = (bf16[256,1024]{1,0:T(8,128)(2,1)}, bf16[256,1024]{1,0:T(8,128)(2,1)S(1)}, u32[]{:S(2)}) copy-start(bf16[256,1024]{1,0:T(8,128)(2,1)S(1)} %copy.83) | copy-start | bytes 1572868
  629.0 8.3 copy-start.16
  629.0 8.3 copy-start.20
  637.3 5.1 copy-start.41
  637.3 5.6 copy-start.42
  637.3 5.6 copy-start.43
  637.3 46.4 %copy-start.6 = (f32[256,1024]{1,0:T(8,128)S(1)}, f32[256,1024]{1,0:T(8,128)}, u32[]{:S(2)}) copy-start(f32[256,1024]{1,0:T(8,128)} %copy-done.5) | copy-start | bytes 3145732
  637.3 46.4 %copy-start.39 = (f32[256]{0:T(256)S(1)}, f32[256]{0:T(256)}, u32[]{:S(2)}) copy-start(f32[256]{0:T(256)} %copy-done.38) | copy-start | bytes 3076
  (10 other events, 11.5 us)
Sparse Core Ops, SparseCore 0:
  11.0 72.3 all-gather.6
  86.4 75.8 all-gather.16
  164.5 45.7 all-gather.8
  212.3 45.8 all-gather.10
  261.1 55.1 all-gather.12
  319.1 76.2 all-gather.14
  533.0 88.1 reduce-scatter.5
  624.1 140.6 reduce-scatter.9
  767.7 183.8 reduce-scatter.11
  954.3 184.3 reduce-scatter.13
  1145.3 153.0 reduce-scatter.7
where the time goes:
time: 1310 us
  waiting for transfers between devices  907 us (69%)
  matrix products  186 us (14%)
  blocking collectives  80.9 us (6%)
  local copies, waits for them, and re-layouts  80.1 us (6%)
  other arithmetic  31.9 us (2%)
  between operations  14.6 us (1%)
    reduce_scatter x1, waiting for transfers between devices, on_device(): lax.psum_scatter(down_term, ('scene', 'blk'), scatter_dimension=0, tiled=...  187 us
    reduce_scatter x1, waiting for transfers between devices, on_device(): lax.psum_scatter(up_term, ('scene', 'blk'), scatter_dimension=0, tiled=True)  187 us
    reduce_scatter x1, waiting for transfers between devices, on_device(): lax.psum_scatter(qkv_term, ('scene', 'blk'), scatter_dimension=0, tiled=T...  160 us
    unnamed x2, blocking collectives  80.9 us
    reduce_scatter x1, waiting for transfers between devices, on_device(): lax.psum_scatter(out_term, ('scene', 'blk'), scatter_dimension=0, tiled=T...  79.7 us
    all_gather x1, waiting for transfers between devices, on_device(): lax.all_gather(w_down, ('scene', 'blk'), axis=0, tiled=True)  70.4 us
    all_gather x1, waiting for transfers between devices, on_device(): lax.all_gather(w_up, ('scene', 'blk'), axis=0, tiled=True)  66.3 us
    reduce_scatter x1, waiting for transfers between devices, on_device(): lax.psum_scatter(pair_rows.astype(jnp.bfloat16), 'blk', scatter_dimension...  57.8 us
  transfers between devices with their start and end apart: 11, of which 10 were waited for; matrix products, arithmetic and copies ran while one was open for 12% of the time, Pallas kernels for 0%

commit v1 on v0

--- a/solution.py
+++ b/solution.py
@@ -1,8 +1,12 @@
+import functools
 import math
 
 import jax
 import jax.numpy as jnp
 from jax import lax
+from jax.experimental import pallas as pl
+from jax.experimental.pallas import tpu as pltpu
+from jax.sharding import Mesh
 from jax.sharding import PartitionSpec as P
 
 D = 1024
@@ -74,7 +78,7 @@
     )
 
 
-def on_device(
+def on_any_slice(
     tokens_in,
     view_heights,
     view_widths,
@@ -272,34 +276,466 @@
     )
 
 
+ALL = ("y", "x", "z", "c")
+LANES = 128
+ROOT = math.sqrt(2.0 / math.pi)
+CUBIC = 0.044715
+
+
+def swap(values, axis, size, distance):
+    return lax.ppermute(values, axis, [(i, i ^ distance) for i in range(size)])
+
+
+def pair(values):
+    return swap(values, "c", 2, 1)
+
+
+def whole(shape):
+    return pl.BlockSpec(shape, lambda *_: (0,) * len(shape))
+
+
+def params(megabytes=60):
+    return pltpu.CompilerParams(vmem_limit_bytes=megabytes * 1024 * 1024)
+
+
+def three_parts(column, lane, first):
+    high = column.astype(jnp.bfloat16).astype(jnp.float32)
+    rest = column - high
+    middle = rest.astype(jnp.bfloat16).astype(jnp.float32)
+    last = rest - middle
+    zero = jnp.zeros_like(last)
+    return jnp.where(
+        lane == first,
+        high,
+        jnp.where(lane == first + 1, middle, jnp.where(lane == first + 2, last, zero)),
+    )
+
+
+def attend_kernel(q_ref, k_ref, v_ref, low_ref, att_ref, aug_ref):
+    lane = lax.broadcasted_iota(jnp.int32, (1, LANES), 1)
+    queries = q_ref[...].astype(jnp.float32) * HEAD_DIM ** (-0.5)
+    keys = k_ref[...]
+    values = v_ref[...].astype(jnp.float32)
+    heads = []
+    for head in range(2):
+        mine = (lane < HEAD_DIM) if head == 0 else (lane >= HEAD_DIM)
+        own_query = jnp.where(mine, queries, 0.0).astype(jnp.bfloat16)
+        scores = against(own_query, keys)
+        highest = jnp.max(scores, axis=1, keepdims=True)
+        expo = jnp.exp(scores - highest).astype(jnp.bfloat16)
+        ones = jnp.where(mine, values, 1.0).astype(jnp.bfloat16)
+        mixed = jnp.dot(expo, ones, preferred_element_type=jnp.float32)
+        heads.append(mixed / pltpu.roll(mixed, HEAD_DIM, 1))
+        log_total = highest + jnp.log(mixed)
+        parts = three_parts(-log_total, lane, HEAD_DIM if head == 0 else 0)
+        aug_ref[head] = jnp.where(mine, queries, parts).astype(jnp.bfloat16)
+    attended = jnp.where(lane < HEAD_DIM, heads[0], heads[1])
+    att_ref[...] = attended
+    low_ref[...] = attended.astype(jnp.bfloat16)
+
+
+def attend(qkv):
+    rows = qkv.shape[0]
+    block = 512
+    return pl.pallas_call(
+        attend_kernel,
+        grid=(rows // block,),
+        in_specs=[
+            pl.BlockSpec((block, LANES), lambda i: (i, 0)),
+            pl.BlockSpec((rows, LANES), lambda i: (0, 1)),
+            pl.BlockSpec((rows, LANES), lambda i: (0, 2)),
+        ],
+        out_specs=[
+            pl.BlockSpec((block, LANES), lambda i: (i, 0)),
+            pl.BlockSpec((block, LANES), lambda i: (i, 0)),
+            pl.BlockSpec((2, block, LANES), lambda i: (0, i, 0)),
+        ],
+        out_shape=[
+            jax.ShapeDtypeStruct((rows, LANES), jnp.bfloat16),
+            jax.ShapeDtypeStruct((rows, LANES), jnp.float32),
+            jax.ShapeDtypeStruct((2, rows, LANES), jnp.bfloat16),
+        ],
+        compiler_params=params(),
+        cost_estimate=pl.CostEstimate(
+            flops=16 * rows * rows * HEAD_DIM, bytes_accessed=16 * rows * LANES, transcendentals=2 * rows * rows
+        ),
+    )(qkv, qkv, qkv)
+
+
+def attend_back_kernel(
+    k_ref, v_ref, aug_ref, do_ref, att_ref, dq_ref, dk_ref, dv_ref, ka_ref, va_ref, kt_ref, dq_acc, dk_acc, dv_acc
+):
+    head, step = pl.program_id(0), pl.program_id(1)
+    rows = k_ref.shape[0]
+    block = do_ref.shape[0]
+    width = 512
+    lane = lax.broadcasted_iota(jnp.int32, (1, LANES), 1)
+    spare = jnp.where(head == 0, HEAD_DIM, 0)
+    mine = (lane < spare) | (lane >= spare + HEAD_DIM)
+
+    @pl.when((head == 0) & (step == 0))
+    def _():
+        kt_ref[...] = k_ref[...].astype(jnp.float32).T.astype(jnp.bfloat16)
+
+    @pl.when(step == 0)
+    def _():
+        ones = jnp.where(lane < spare + 3, 1.0, 0.0)
+        ka_ref[...] = jnp.where(mine, k_ref[...].astype(jnp.float32), ones).astype(jnp.bfloat16)
+        va_ref[...] = jnp.where(mine, v_ref[...].astype(jnp.float32), ones).astype(jnp.bfloat16)
+        dk_acc[head] = jnp.zeros((rows, LANES), jnp.float32)
+        dv_acc[head] = jnp.zeros((rows, LANES), jnp.float32)
+
+    delta = do_ref[...].astype(jnp.float32)
+    probe = jnp.sum(jnp.where(mine, delta * att_ref[...], 0.0), axis=1, keepdims=True)
+    own_delta = jnp.where(mine, delta, three_parts(-probe, lane, spare)).astype(jnp.bfloat16)
+    own_query = aug_ref[0]
+    total = jnp.zeros((LANES, block), jnp.float32)
+    for first in range(0, rows, width):
+        part = slice(first, first + width)
+        probs = jnp.exp(against(ka_ref[part, :], own_query))
+        score_delta = (probs * against(va_ref[part, :], own_delta)).astype(jnp.bfloat16)
+        dv_acc[head, part, :] += jnp.dot(
+            probs.astype(jnp.bfloat16), own_delta, preferred_element_type=jnp.float32
+        )
+        dk_acc[head, part, :] += jnp.dot(score_delta, own_query, preferred_element_type=jnp.float32)
+        total += jnp.dot(kt_ref[:, part], score_delta, preferred_element_type=jnp.float32)
+    query_delta = (total * HEAD_DIM ** (-0.5)).T
+    place = pl.ds(pl.multiple_of(step * block, block), block)
+
+    @pl.when(head == 0)
+    def _():
+        dq_acc[place, :] = query_delta
+
+    @pl.when(head == 1)
+    def _():
+        dq_ref[place, :] = jnp.where(lane < HEAD_DIM, dq_acc[place, :], query_delta).astype(jnp.bfloat16)
+
+    @pl.when((head == 1) & (step == pl.num_programs(1) - 1))
+    def _():
+        dk_ref[...] = jnp.where(lane < HEAD_DIM, dk_acc[0], dk_acc[1]).astype(jnp.bfloat16)
+        dv_ref[...] = jnp.where(lane < HEAD_DIM, dv_acc[0], dv_acc[1]).astype(jnp.bfloat16)
+
+
+def attend_back(qkv, augmented, delta, attended):
+    rows = qkv.shape[0]
+    block = 256
+    shape = jax.ShapeDtypeStruct((rows, LANES), jnp.bfloat16)
+    return pl.pallas_call(
+        attend_back_kernel,
+        grid=(2, rows // block),
+        in_specs=[
+            pl.BlockSpec((rows, LANES), lambda h, i: (0, 1)),
+            pl.BlockSpec((rows, LANES), lambda h, i: (0, 2)),
+            pl.BlockSpec((1, block, LANES), lambda h, i: (h, i, 0)),
+            pl.BlockSpec((block, LANES), lambda h, i: (i, 0)),
+            pl.BlockSpec((block, LANES), lambda h, i: (i, 0)),
+        ],
+        out_specs=[whole((rows, LANES))] * 3,
+        out_shape=[shape] * 3,
+        scratch_shapes=[
+            pltpu.VMEM((rows, LANES), jnp.bfloat16),
+            pltpu.VMEM((rows, LANES), jnp.bfloat16),
+            pltpu.VMEM((LANES, rows), jnp.bfloat16),
+            pltpu.VMEM((rows, LANES), jnp.float32),
+            pltpu.VMEM((2, rows, LANES), jnp.float32),
+            pltpu.VMEM((2, rows, LANES), jnp.float32),
+        ],
+        compiler_params=params(),
+        cost_estimate=pl.CostEstimate(
+            flops=40 * rows * rows * HEAD_DIM, bytes_accessed=20 * rows * LANES, transcendentals=2 * rows * rows
+        ),
+    )(qkv, qkv, augmented, delta, attended)
+
+
+def mlp_kernel(core_ref, nt_ref, og_ref, up_ref, down_ref, act_ref, ud_ref, lo_ref, ntd_ref):
+    step = pl.program_id(0)
+    wide = up_ref.shape[0] * up_ref.shape[1]
+    w_up = up_ref[...].reshape(wide, up_ref.shape[2])
+    w_down = down_ref[...].reshape(down_ref.shape[0] * down_ref.shape[2], down_ref.shape[3])
+    upward = jnp.dot(nt_ref[...], w_up, preferred_element_type=jnp.float32)
+    curve = jnp.tanh(ROOT * (upward + CUBIC * upward * upward * upward))
+    active = (0.5 * upward * (1.0 + curve)).astype(jnp.bfloat16)
+    slope = 0.5 * (1.0 + curve) + 0.5 * upward * (1.0 - curve * curve) * (
+        ROOT * (1.0 + 3.0 * CUBIC * upward * upward)
+    )
+    delta = (against(og_ref[...], w_down) * slope).astype(jnp.bfloat16)
+    act_ref[...] = active
+    ud_ref[...] = delta
+    lo = jnp.dot(active, w_down, preferred_element_type=jnp.float32)
+    ntd = against(delta, w_up)
+
+    @pl.when(step == 0)
+    def _():
+        lo_ref[...] = lo
+        ntd_ref[...] = ntd
+
+    @pl.when(step > 0)
+    def _():
+        lo_ref[...] += lo
+        ntd_ref[...] += ntd
+
+
+def mlp(core, normed, out_grad, weights):
+    rows = normed.shape[0]
+    devices, tall, width = weights.shape
+    chips = devices // 2
+    steps = 2
+    by_core = weights.reshape(chips, 2, tall, width)
+    grid_spec = pltpu.PrefetchScalarGridSpec(
+        num_scalar_prefetch=1,
+        grid=(steps,),
+        in_specs=[
+            pl.BlockSpec((rows, D), lambda k, core: (0, 0)),
+            pl.BlockSpec((rows, D), lambda k, core: (0, 0)),
+            pl.BlockSpec((devices, 32, width), lambda k, core: (0, 5 + 2 * core[0] + k, 0)),
+            pl.BlockSpec((chips // steps, 1, 128, width), lambda k, core: (k, core[0], 0, 0)),
+        ],
+        out_specs=[
+            pl.BlockSpec((rows, width), lambda k, core: (0, k)),
+            pl.BlockSpec((rows, width), lambda k, core: (0, k)),
+            pl.BlockSpec((rows, D), lambda k, core: (0, 0)),
+            pl.BlockSpec((rows, D), lambda k, core: (0, 0)),
+        ],
+    )
+    return pl.pallas_call(
+        mlp_kernel,
+        grid_spec=grid_spec,
+        out_shape=[
+            jax.ShapeDtypeStruct((rows, steps * width), jnp.bfloat16),
+            jax.ShapeDtypeStruct((rows, steps * width), jnp.bfloat16),
+            jax.ShapeDtypeStruct((rows, D), jnp.float32),
+            jax.ShapeDtypeStruct((rows, D), jnp.float32),
+        ],
+        compiler_params=params(),
+        cost_estimate=pl.CostEstimate(
+            flops=8 * rows * D * steps * width, bytes_accessed=16 * 1024 * 1024, transcendentals=rows * steps * width
+        ),
+    )(core, normed, out_grad, weights, by_core)
+
+
+def reorder_kernel(index_ref, in_ref, out_ref):
+    blocks = in_ref.shape[0]
+    for block in range(blocks):
+        out_ref[block ^ index_ref[0]] = in_ref[block]
+
+
+def reorder(index, blocks):
+    return pl.pallas_call(
+        reorder_kernel,
+        in_specs=[pl.BlockSpec(memory_space=pltpu.SMEM), whole(blocks.shape)],
+        out_specs=whole(blocks.shape),
+        out_shape=jax.ShapeDtypeStruct(blocks.shape, blocks.dtype),
+        compiler_params=params(),
+    )(index.reshape(1).astype(jnp.int32), blocks)
+
+
+def moments(values):
+    centred = values - jnp.mean(values, axis=1, keepdims=True)
+    scale = lax.rsqrt(jnp.mean(centred * centred, axis=1, keepdims=True) + EPSILON)
+    return centred * scale, scale
+
+
+def norm_back(delta, gain, normal, scale):
+    e = delta * gain
+    return scale * (
+        e - jnp.mean(e, axis=1, keepdims=True) - normal * jnp.mean(e * normal, axis=1, keepdims=True)
+    )
+
+
+def scatter_sum(parts, first, second, places):
+    for axis in (first, second):
+        dim = 0 if (axis == "y" or parts.ndim < 5) else 1
+        send = lax.dynamic_index_in_dim(parts, 1 - places[axis], dim, keepdims=False)
+        keep = lax.dynamic_index_in_dim(parts, places[axis], dim, keepdims=False)
+        parts = (keep.astype(jnp.float32) + swap(send, axis, 2, 1).astype(jnp.float32)).astype(jnp.bfloat16)
+    count = parts.shape[0]
+    total = lax.dynamic_index_in_dim(parts, places["z"], 0, keepdims=False).astype(jnp.float32)
+    for far in range(1, count):
+        send = lax.dynamic_index_in_dim(parts, places["z"] ^ far, 0, keepdims=False)
+        total = total + swap(send, "z", count, far).astype(jnp.float32)
+    return total
+
+
+def on_planes(
+    tokens_in,
+    out_grad,
+    w_qkv,
+    w_out,
+    w_up,
+    w_down,
+    norm1_gain,
+    norm1_bias,
+    norm2_gain,
+    norm2_bias,
+):
+    depth = lax.axis_size("z")
+    blocks = 2 * depth
+    chips = 4 * depth
+    rows = tokens_in.shape[0]
+    share = w_qkv.shape[0]
+    low = jnp.bfloat16
+    places = {axis: lax.axis_index(axis) for axis in ALL}
+    core = places["c"]
+    block = 2 * places["z"] + core
+    device = ((2 * places["y"] + places["x"]) * depth + places["z"]) * 2 + core
+
+    up_rows = w_up.reshape(share, chips, 2, LANES).transpose(0, 2, 1, 3).reshape(share, 4, D)
+    up_rows = up_rows.transpose(1, 0, 2).reshape(4 * share, D)
+    weights = lax.all_gather(jnp.concatenate([w_down, w_out, up_rows], axis=0), ALL, axis=0)
+
+    by_block = w_qkv.reshape(share, 3, blocks, LANES).transpose(2, 0, 1, 3).reshape(blocks, share, 3 * LANES)
+    near = reorder(block, by_block).reshape(depth, 2, share, 3 * LANES)
+    pieces = jnp.stack([near[:, 0], pair(near[:, 1])], axis=1)
+    along = jnp.stack([pieces[0]] + [swap(pieces[far], "z", depth, far) for far in range(1, depth)])
+    across = jnp.stack([along] + [swap(along, ("y", "x"), 4, far) for far in range(1, 4)])
+    own_qkv = reorder(device, across.reshape(2 * chips, share, 3 * LANES)).reshape(D, 3 * LANES)
+
+    gains = jnp.stack([norm1_gain, norm1_bias, norm2_gain, norm2_bias]).reshape(1, 4 * share)
+    gains = jnp.concatenate([gains, pair(gains)])
+    gains = jnp.concatenate([gains] + [swap(gains, "z", depth, far) for far in range(1, depth)])
+    gains = jnp.concatenate([gains] + [swap(gains, ("y", "x"), 4, far) for far in range(1, 4)])
+    order = device ^ jnp.arange(2 * chips, dtype=jnp.int32)
+    chosen = (order[:, None] == jnp.arange(2 * chips, dtype=jnp.int32)[None, :]).astype(low)
+    gains = jnp.dot(chosen, gains, preferred_element_type=jnp.float32)
+    gains = gains.reshape(2 * chips, 4, share).transpose(1, 0, 2).reshape(4, D)
+    gain_one, bias_one, gain_two, bias_two = (gains[i] for i in range(4))
+
+    far_tokens = [tokens_in] + [swap(tokens_in, "z", depth, far) for far in range(1, depth)]
+    group = jnp.concatenate([part for mine in far_tokens for part in (mine, pair(mine))])
+    grads = jnp.concatenate([out_grad, pair(out_grad)])
+
+    normal_group, _ = moments(group.astype(jnp.float32))
+    normed = (normal_group * gain_one + bias_one).astype(low)
+    qkv = jnp.dot(normed, own_qkv, preferred_element_type=jnp.float32).astype(low)
+    attended_low, attended, augmented = attend(qkv)
+
+    both = 2 * rows
+    sides = [attended_low[:both]] + [
+        swap(attended_low[far * both : (far + 1) * both], "z", depth, far) for far in range(1, depth)
+    ]
+    own_heads = jnp.concatenate(sides, axis=1)
+    other_heads = pair(own_heads)
+    other_heads = jnp.concatenate([other_heads[rows:], other_heads[:rows]])
+    all_heads = jnp.concatenate([own_heads, other_heads], axis=1)
+
+    full_out = weights[:, w_down.shape[0] : w_down.shape[0] + share].reshape(blocks, LANES, D)
+    near_out = reorder(block, full_out).reshape(depth, 2, LANES, D).transpose(1, 0, 2, 3)
+    own_out = near_out[0].reshape(depth * LANES, D)
+    inputs = tokens_in.astype(jnp.float32)
+    hidden = inputs + jnp.dot(
+        all_heads[:rows], near_out.reshape(D, D), preferred_element_type=jnp.float32
+    )
+    normal_two, scale_two = moments(hidden)
+    normed_two = (normal_two * gain_two + bias_two).astype(low)
+    normed_both = jnp.concatenate([normed_two, pair(normed_two)])
+
+    active, up_delta, out_part, two_part = mlp(core.reshape(1), normed_both, grads, weights)
+    result = (hidden + out_part[:rows] + pair(out_part[rows:])).astype(low)
+    norm_two_delta = two_part[:rows] + pair(two_part[rows:])
+    gain_two_part = jnp.sum(norm_two_delta * normal_two, axis=0)
+    bias_two_part = jnp.sum(norm_two_delta, axis=0)
+    hidden_delta = out_grad.astype(jnp.float32) + norm_back(norm_two_delta, gain_two, normal_two, scale_two)
+    hidden_low = hidden_delta.astype(low)
+    hidden_both = jnp.concatenate([hidden_low, pair(hidden_low)])
+
+    att_delta = against(hidden_both, own_out).astype(low)
+    far_delta = [att_delta[:, :LANES]] + [
+        swap(att_delta[:, far * LANES : (far + 1) * LANES], "z", depth, far) for far in range(1, depth)
+    ]
+
+    half = D // 2
+    out_cols = lax.dynamic_slice_in_dim(hidden_both, core * half, half, 1)
+    out_term = outer(all_heads, out_cols).astype(low).reshape(2, depth, LANES, half).transpose(1, 0, 2, 3)
+    out_term = reorder(block, out_term.reshape(blocks, LANES, half)).reshape(2, 2, depth, D // chips, half)
+    up_term = outer(normed_both, up_delta).astype(low).reshape(2, 2, depth, D // chips, up_delta.shape[1])
+    down_term = outer(active, grads).astype(low).reshape(2, 2, depth, w_down.shape[0], D)
+    first_sum = scatter_sum(jnp.concatenate([up_term, out_term], axis=4), "y", "x", places)
+    down_sum = scatter_sum(down_term, "x", "y", places)
+
+    query_delta, key_delta, value_delta = attend_back(qkv, augmented, jnp.concatenate(far_delta), attended)
+    qkv_delta = jnp.concatenate([query_delta, key_delta, value_delta], axis=1)
+    one_part = against(qkv_delta, own_qkv)
+    gain_one_part = jnp.sum(one_part * normal_group, axis=0)
+    bias_one_part = jnp.sum(one_part, axis=0)
+    one_part = one_part.reshape(depth, 2, rows, D)
+    one_sum = one_part[:, 0] + pair(one_part[:, 1].astype(low)).astype(jnp.float32)
+    norm_one_delta = one_sum[0]
+    for far in range(1, depth):
+        norm_one_delta = norm_one_delta + swap(one_sum[far].astype(low), "z", depth, far).astype(jnp.float32)
+    normal_one, scale_one = moments(inputs)
+    input_grad = hidden_delta + norm_back(norm_one_delta, gain_one, normal_one, scale_one)
+
+    def halves(vectors):
+        high = vectors.astype(low)
+        return jnp.concatenate([high, (vectors - high.astype(jnp.float32)).astype(low)])
+
+    tall = D // 4
+    vectors = jnp.stack([gain_one_part, bias_one_part, gain_two_part, bias_two_part])
+    vectors = halves(vectors).reshape(8, 4, tall).transpose(1, 0, 2)
+    vectors = jnp.pad(vectors, ((0, 0), (0, 8), (0, 3 * LANES - tall)))
+    qkv_term = outer(normed, qkv_delta).astype(low).reshape(4, tall, 3 * LANES)
+    qkv_term = jnp.concatenate([qkv_term, vectors], axis=1)
+    plane = 2 * places["y"] + places["x"]
+    qkv_term = reorder(plane, qkv_term)
+    quarter = qkv_term[0].astype(jnp.float32)
+    for far in range(1, 4):
+        quarter = quarter + swap(qkv_term[far], ("y", "x"), 4, far).astype(jnp.float32)
+    vectors = halves(quarter[tall : tall + 4] + quarter[tall + 4 : tall + 8])
+    vectors = jnp.pad(vectors, ((0, 8), (0, 0)))
+    quarter = reorder(places["z"], quarter[:tall].astype(low).reshape(depth, 2 * share, 3 * LANES))
+    quarter = jnp.concatenate([quarter, jnp.broadcast_to(vectors[None], (depth, 16, 3 * LANES))], axis=1)
+    sides = [quarter[0]] + [swap(quarter[far], "z", depth, far) for far in range(1, depth)]
+    vectors = sum(side[2 * share :].astype(jnp.float32) for side in sides)
+    vectors = halves(vectors[:4] + vectors[4:8])
+    vectors = jnp.pad(vectors, ((0, 8), (0, 0)))
+    sides = jnp.stack([side[: 2 * share].reshape(2, share, 3 * LANES) for side in sides])
+    sides = reorder(core, sides.transpose(1, 0, 2, 3))
+    send = jnp.concatenate([sides[1].reshape(depth * share, 3 * LANES), vectors])
+    got = pair(send)
+    vectors = vectors.astype(jnp.float32) + got[depth * share :].astype(jnp.float32)
+    vectors = lax.dynamic_slice_in_dim(vectors[:4] + vectors[4:8], (places["z"] * 2 + core) * share, share, 1)
+    parts = jnp.stack([sides[0], got[: depth * share].reshape(depth, share, 3 * LANES)], axis=1)
+    parts = reorder(block, parts.reshape(blocks, share, 3 * LANES)).reshape(blocks, share, 3, LANES)
+    qkv_grad = parts.transpose(1, 2, 0, 3).reshape(share, 3 * D).astype(jnp.float32)
+
+    mine = lax.dynamic_slice_in_dim(first_sum, core * share, share, 0)
+    others = pair(lax.dynamic_slice_in_dim(first_sum, (1 - core) * share, share, 0))
+    both_cores = jnp.where(core == 0, jnp.stack([mine, others]), jnp.stack([others, mine]))
+    wide = up_delta.shape[1]
+    up_grad = both_cores[:, :, :wide].reshape(2, share, chips, LANES).transpose(1, 2, 0, 3).reshape(share, 2 * wide)
+    out_weight_grad = both_cores[:, :, wide:].transpose(1, 0, 2).reshape(share, D)
+    return (
+        result,
+        input_grad,
+        qkv_grad,
+        out_weight_grad,
+        up_grad,
+        down_sum,
+        vectors[0],
+        vectors[1],
+        vectors[2],
+        vectors[3],
+    )
+
+
 def solution(mesh):
-    in_specs = (
-        P(("scene", "blk"), None),
-        P("scene", None),
-        P("scene", None),
-        P("scene", None),
-        P(("scene", "blk"), None),
-        P(("scene", "blk"), None),
-        P(("scene", "blk"), None),
-        P(("scene", "blk"), None),
-        P(("scene", "blk"), None),
-        P(("scene", "blk")),
-        P(("scene", "blk")),
-        P(("scene", "blk")),
-        P(("scene", "blk")),
-    )
-    out_specs = (
-        P(("scene", "blk"), None),
-        P(("scene", "blk"), None),
-        P(("scene", "blk"), None),
-        P(("scene", "blk"), None),
-        P(("scene", "blk"), None),
-        P(("scene", "blk"), None),
-        P(("scene", "blk")),
-        P(("scene", "blk")),
-        P(("scene", "blk")),
-        P(("scene", "blk")),
-    )
-    return jax.shard_map(
-        on_device, mesh=mesh, in_specs=in_specs, out_specs=out_specs, check_vma=False
-    )
+    scenes, blocks = mesh.devices.shape
+
+    def place(axes):
+        matrix = P(axes, None)
+        views = P(axes[: len(axes) // 2] if len(axes) > 2 else axes[0], None)
+        vector = P(axes)
+        ins = (matrix, views, views, views, matrix, matrix, matrix, matrix, matrix) + (vector,) * 4
+        return ins, (matrix,) * 6 + (vector,) * 4
+
+    def run(*arrays):
+        one_scene = arrays[1].shape[1] == 4
+        if scenes == 4 and blocks == 8 and one_scene and arrays[0].shape[0] == 8192:
+            fine = Mesh(mesh.devices.reshape(2, 2, blocks // 2, 2), ALL)
+            ins, outs = place(ALL)
+            step = lambda tokens, heights, widths, labels, *rest: on_planes(tokens, *rest)
+            return jax.shard_map(step, mesh=fine, in_specs=ins, out_specs=outs, check_vma=False)(*arrays)
+        ins, outs = place(("scene", "blk"))
+        return jax.shard_map(on_any_slice, mesh=mesh, in_specs=ins, out_specs=outs, check_vma=False)(*arrays)
+
+    return run

time: 1310 us -> 524 us (0.40)
  waiting for transfers between devices: 907 us -> 233 us
  matrix products: 186 us -> 23.6 us
  blocking collectives: 80.9 us -> 0 us
  Pallas kernels: 0 us -> 79.3 us
  starting transfers between devices: 0.44 us -> 73.9 us
  local copies, waits for them, and re-layouts: 80.1 us -> 52.8 us
    reduce_scatter x5 -> x0, waiting for transfers between devices: 671 us -> none  [the longest x1 187 us: on_device(): lax.psum_scatter(down_term, ('scene', 'blk'), scatter_dimension=0, tiled=...]
    all_gather x6 -> x1, waiting for transfers between devices: 233 us -> 0.01 us  [on_planes(): lax.all_gather(jnp.concatenate([w_down, w_out, up_rows], axis=0), ALL, ax...]
    ppermute x0 -> x55, waiting for transfers between devices: none -> 233 us  [swap(): return lax.ppermute(values, axis, [(i, i ^ distance) for i in range(size)])]
    dot_general x18 -> x3, matrix products: 138 us -> 4.56 us  [the longest x1 3.56 us: on_planes(): jnp.dot(normed, own_qkv, preferred_element_type=jnp.float32).astype(low)]
    unnamed x2 -> x0, blocking collectives: 80.9 us -> none
    pallas_call x0 -> x11, Pallas kernels: none -> 79.3 us  [the longest x1 30 us: attend_back(): pl.pallas_call(attend_back_kernel, grid=(2, rows // block), in_specs=[pl....]
    ppermute x0 -> x55, starting transfers between devices: none -> 73.9 us  [swap(): return lax.ppermute(values, axis, [(i, i ^ distance) for i in range(size)])]
    dynamic_update_slice x4 -> x0, local copies, waits for them, and re-layouts: 22.5 us -> none  [on_device(): lax.scan(joint_step, query_start, (jnp.arange(block_count, dtype=jnp.int3...]
  transfers between devices with their start and end apart: 11 -> 56, of which waited for: 10 -> 20; matrix products, arithmetic and copies ran while one was open for 12% -> 20% of each run, Pallas kernels for 0% -> 12%
where the time goes in v1:
time: 524 us; the launch traced here: 519 us
  waiting for transfers between devices  233 us (44%)
  Pallas kernels  79.3 us (15%)
  starting transfers between devices  73.9 us (14%)
  local copies, waits for them, and re-layouts  52.8 us (10%)
  other arithmetic  40.9 us (8%)
  matrix products  23.6 us (5%)
  between operations  15.1 us (3%)
    ppermute x55, waiting for transfers between devices, swap(): return lax.ppermute(values, axis, [(i, i ^ distance) for i in range(size)])  233 us
    ppermute x55, starting transfers between devices, swap(): return lax.ppermute(values, axis, [(i, i ^ distance) for i in range(size)])  73.9 us
    pallas_call x1, Pallas kernels, attend_back(): pl.pallas_call(attend_back_kernel, grid=(2, rows // block), in_specs=[pl....  30 us
    pallas_call x1, Pallas kernels, attend(): pl.pallas_call(attend_kernel, grid=(rows // block,), in_specs=[pl.BlockSp...  17.2 us
    unnamed x85, local copies, waits for them, and re-layouts  16 us
    pallas_call x1, Pallas kernels, mlp(): pl.pallas_call(mlp_kernel, grid_spec=grid_spec, out_shape=[jax.ShapeDtype...  16 us
    pallas_call x8, Pallas kernels, reorder(): pl.pallas_call(reorder_kernel, in_specs=[pl.BlockSpec(memory_space=pltpu....  16 us
    dot_general x4, matrix products, outer(): lax.dot_general(left, right, (((0,), (0,)), ((), ())), preferred_element_...  13.5 us
  transfers between devices with their start and end apart: 56, of which 20 were waited for; matrix products, arithmetic and copies ran while one was open for 20% of the time, Pallas kernels for 12%

profile of v1, /device:TPU:0, one launch (start us, length us, event | category | flops | bytes accessed | tf_op | source)
XLA Modules:
  0.0 518.9 jit_solution(12653840436657084219)
XLA Ops:
  14.7 2.7 collective-permute-start.1
  18.6 2.8 collective-permute-start.17
  21.6 21.7 %collective-permute-done.15 = bf16[2,32,384]{2,1,0:T(8,128)(2,1)S(1)} collective-permute-done((bf16[2,32,384]{2,1,0:T(8,128)(2,1)S(1)}, bf16[2,32,384]{2,1,0:T(8,128)(2,1)S(1)}, u32[]{:S(2)}, u32[]{:S(2)}) %collective-permute-start.15) | collective-permute-done | bytes 49184 | tf_op jit(solution)/shard_map/ppermute | solution.py:286
  44.1 2.3 collective-permute-start.19
  46.4 5.4 %collective-permute-start.10 = (bf16[2,128]{1,0:T(2,128)(2,1)S(1)}, bf16[2,128]{1,0:T(2,128)(2,1)S(1)}, u32[]{:S(2)}, u32[]{:S(2)}) collective-permute-start(bf16[2,128]{1,0:T(2,128)(2,1)S(1)} %pad_maximum_fusion.14), channel_id=1, source_target_pairs={{0,6},{2,4},{4,2},{6,0},{1,7},{3,5},{5,3},{7,1},{8,14},{10,12},{12... | collective-permute-start | bytes 1544 | tf_op jit(solution)/shard_map/ppermute | solution.py:286
  53.3 3.7 collective-permute-done.9
  57.8 2.1 collective-permute-start.12
  66.7 7.5 %collective-permute-done.18 = bf16[4,2,32,384]{3,2,1,0:T(8,128)(2,1)S(1)} collective-permute-done((bf16[4,2,32,384]{3,2,1,0:T(8,128)(2,1)}, bf16[4,2,32,384]{3,2,1,0:T(8,128)(2,1)S(1)}, u32[]{:S(2)}, u32[]{:S(2)}) %collective-permute-start.18) | collective-permute-done | bytes 196640 | tf_op jit(solution)/shard_map/ppermute | solution.py:286
  75.6 38.9 %collective-permute-done.3 = bf16[256,1024]{1,0:T(8,128)(2,1)S(1)} collective-permute-done((bf16[256,1024]{1,0:T(8,128)(2,1)S(1)}, bf16[256,1024]{1,0:T(8,128)(2,1)S(1)}, u32[]{:S(2)}, u32[]{:S(2)}) %collective-permute-start.3) | collective-permute-done | bytes 524320 | tf_op jit(solution)/shard_map/ppermute | solution.py:286
  114.4 2.1 pad_maximum_fusion.3
  116.5 2.1 shard_map.178
  125.1 3.0 convert_reduce_fusion
  131.8 2.0 copy-done.8
  133.8 3.6 convolution_convert_fusion.2.q_ref.k_ref.v_ref
  137.3 17.2 %shard_map.179 = (bf16[2048,128]{1,0:T(8,128)(2,1)}, f32[2048,128]{1,0:T(8,128)}, bf16[2,2048,128]{2,1,0:T(8,128)(2,1)}) custom-call(bf16[2048,384]{1,0:T(8,128)(2,1)} %convolution_convert_fusion.2.q_ref.k_ref.v_ref, bf16[2048,384]{1,0:T(8,128)(2,1)} %convolution_convert_fusion.2.q_ref.k_ref.v_ref, bf16[2048,384]{1,0:T(8,128)(2,1)} %convolution_convert_fusion.2.q_ref.k_ref.v_ref), custom_call_target="tpu_custom_call" | custom-call | flops 4294967296 | bytes 4194304 | tf_op jit(solution)/shard_map/pallas_call | solution.py:340
  154.6 1.9 fusion.74
  157.7 19.9 %collective-permute-start.22 = (bf16[512,128]{1,0:T(8,128)(2,1)S(1)}, bf16[512,128]{1,0:T(8,128)(2,1)S(1)}, u32[]{:S(2)}, u32[]{:S(2)}) collective-permute-start(bf16[512,128]{1,0:T(8,128)(2,1)S(1)} %get-tuple-element.78), channel_id=1, source_target_pairs={{0,4},{2,6},{4,0},{6,2},{1,5},{3,7},{5,1},{7,3},{8,12},{10,14},{12... | collective-permute-start | bytes 393224 | tf_op jit(solution)/shard_map/ppermute | solution.py:286
  177.6 9.6 %collective-permute-done.22 = bf16[512,128]{1,0:T(8,128)(2,1)S(1)} collective-permute-done((bf16[512,128]{1,0:T(8,128)(2,1)S(1)}, bf16[512,128]{1,0:T(8,128)(2,1)S(1)}, u32[]{:S(2)}, u32[]{:S(2)}) %collective-permute-start.22) | collective-permute-done | bytes 131104 | tf_op jit(solution)/shard_map/ppermute | solution.py:286
  191.0 3.3 slice.286
  194.3 3.0 shard_map.180
  203.8 16.0 %shard_map.181 = (bf16[512,2048]{1,0:T(8,128)(2,1)}, bf16[512,2048]{1,0:T(8,128)(2,1)}, f32[512,1024]{1,0:T(8,128)}, f32[512,1024]{1,0:T(8,128)}) custom-call(s32[1]{0:T(128)} %bitcast.31.core_ref.index_ref, bf16[512,1024]{1,0:T(8,128)(2,1)} %pad_maximum_fusion.2.nt_ref, bf16[512,1024]{1,0:T(8,128)(2,1)} %copy-done.12, bf16[32,288,1024]{2,1,0:T(8,128)(2,1)} %bitcast.207, ...), custom_call_target="tpu_custom_call" | custom-call | flops 8589934592 | bytes 16777216 | tf_op jit(solution)/shard_map/pallas_call | solution.py:500
  224.0 1.9 multiply_reduce_fusion
  228.5 2.4 convolution_convert_fusion
  237.2 3.2 collective-permute-start.30
  240.4 4.5 convolution_convert_fusion.1
  244.9 4.0 collective-permute-done.31
  249.7 30.0 %shard_map.182 = (bf16[2048,128]{1,0:T(8,128)(2,1)}, bf16[2048,128]{1,0:T(8,128)(2,1)}, bf16[2048,128]{1,0:T(8,128)(2,1)}) custom-call(bf16[2048,384]{1,0:T(8,128)(2,1)} %convolution_convert_fusion.2.q_ref.k_ref.v_ref, bf16[2048,384]{1,0:T(8,128)(2,1)} %convolution_convert_fusion.2.q_ref.k_ref.v_ref, bf16[2,2048,128]{2,1,0:T(8,128)(2,1)} %get-tuple-element.23.aug_ref, ...), custom_call_target="tpu_custom_call" | custom-call | flops 10737418240 | bytes 5242880 | tf_op jit(solution)/shard_map/pallas_call | solution.py:423
  283.3 4.7 convolution_convert_fusion.4
  288.0 4.8 fusion.6
  293.8 2.1 shard_map.183
  295.9 1.9 slice_bitcast_fusion.6
  298.3 2.4 collective-permute-start.39
  301.4 2.0 convolution_convert_fusion.3
  304.5 2.3 shard_map.187
  306.7 4.0 collective-permute-done.39
  316.5 2.0 collective-permute-start.41
  318.6 2.3 collective-permute-start.42
  320.9 3.3 fusion.12
  328.2 2.6 fusion.10
  332.5 3.8 fusion.16
  336.9 65.9 %collective-permute-done.51 = bf16[4,128,1024]{2,1,0:T(8,128)(2,1)S(1)} collective-permute-done((bf16[4,128,1024]{2,1,0:T(8,128)(2,1)S(1)}, bf16[4,128,1024]{2,1,0:T(8,128)(2,1)S(1)}, u32[]{:S(2)}, u32[]{:S(2)}) %collective-permute-start.51) | collective-permute-done | bytes 1048608 | tf_op jit(solution)/shard_map/ppermute | solution.py:286
  407.8 2.5 fusion.8
  419.0 8.1 %collective-permute-done.53 = bf16[128,1024]{1,0:T(8,128)(2,1)} collective-permute-done((bf16[128,1024]{1,0:T(8,128)(2,1)S(1)}, bf16[128,1024]{1,0:T(8,128)(2,1)}, u32[]{:S(2)}, u32[]{:S(2)}) %collective-permute-start.53) | collective-permute-done | bytes 262176 | tf_op jit(solution)/shard_map/ppermute | solution.py:286
  427.1 2.1 fusion.39
  429.2 3.7 fusion.69
  442.5 17.9 %collective-permute-done.34 = bf16[256,1024]{1,0:T(8,128)(2,1)S(1)} collective-permute-done((bf16[256,1024]{1,0:T(8,128)(2,1)S(1)}, bf16[256,1024]{1,0:T(8,128)(2,1)S(1)}, u32[]{:S(2)}, u32[]{:S(2)}) %collective-permute-start.34) | collective-permute-done | bytes 524320 | tf_op jit(solution)/shard_map/ppermute | solution.py:286
  460.5 36.7 %collective-permute-done.35 = bf16[256,1024]{1,0:T(8,128)(2,1)S(1)} collective-permute-done((bf16[256,1024]{1,0:T(8,128)(2,1)S(1)}, bf16[256,1024]{1,0:T(8,128)(2,1)S(1)}, u32[]{:S(2)}, u32[]{:S(2)}) %collective-permute-start.35) | collective-permute-done | bytes 524320 | tf_op jit(solution)/shard_map/ppermute | solution.py:286
  497.8 9.7 %collective-permute-done.47 = bf16[64,2560]{1,0:T(8,128)(2,1)S(1)} collective-permute-done((bf16[64,2560]{1,0:T(8,128)(2,1)S(1)}, bf16[64,2560]{1,0:T(8,128)(2,1)S(1)}, u32[]{:S(2)}, u32[]{:S(2)}) %collective-permute-start.47) | collective-permute-done | bytes 327712 | tf_op jit(solution)/shard_map/ppermute | solution.py:286
  (281 shorter events, 102.2 us)
Async XLA Ops:
  7.2 183.8 %all-gather.3.cloned.1.call-start = ((), (), s32[]{:S(2)}) async-start(), calls=%async_computation | async-start | bytes 19464192 | tf_op jit(solution)/shard_map/all_gather | solution.py:584
  14.7 60.3 %collective-permute-start.1 = (bf16[256,1024]{1,0:T(8,128)(2,1)S(1)}, bf16[256,1024]{1,0:T(8,128)(2,1)S(1)}, u32[]{:S(2)}, u32[]{:S(2)}) collective-permute-start(bf16[256,1024]{1,0:T(8,128)(2,1)S(1)} %copy-done.2), channel_id=1, source_target_pairs={{0,2},{2,0},{4,6},{6,4},{1,3},{3,1},{5,7},{7,5},{8,10},{10,8},{12,... | collective-permute-start | bytes 1572872 | tf_op jit(solution)/shard_map/ppermute | solution.py:286
  17.4 26.0 %collective-permute-start.15 = (bf16[2,32,384]{2,1,0:T(8,128)(2,1)S(1)}, bf16[2,32,384]{2,1,0:T(8,128)(2,1)S(1)}, u32[]{:S(2)}, u32[]{:S(2)}) collective-permute-start(bf16[2,32,384]{2,1,0:T(8,128)(2,1)S(1)} %get-tuple-element.88), channel_id=1, source_target_pairs={{0,2},{2,0},{4,6},{6,4},{1,3},{3,1},{5,7},{7,5},{8,10},{10,8},{12,... | collective-permute-start | bytes 147464 | tf_op jit(solution)/shard_map/ppermute | solution.py:286
  18.6 24.7 %collective-permute-start.17 = (bf16[2,32,384]{2,1,0:T(8,128)(2,1)S(1)}, bf16[2,32,384]{2,1,0:T(8,128)(2,1)S(1)}, u32[]{:S(2)}, u32[]{:S(2)}) collective-permute-start(bf16[2,32,384]{2,1,0:T(8,128)(2,1)S(1)} %get-tuple-element.89), channel_id=1, source_target_pairs={{0,6},{2,4},{4,2},{6,0},{1,7},{3,5},{5,3},{7,1},{8,14},{10,12},{12... | collective-permute-start | bytes 147464 | tf_op jit(solution)/shard_map/ppermute | solution.py:286
  21.5 21.9 %collective-permute-start.16 = (bf16[2,32,384]{2,1,0:T(8,128)(2,1)S(1)}, bf16[2,32,384]{2,1,0:T(8,128)(2,1)S(1)}, u32[]{:S(2)}, u32[]{:S(2)}) collective-permute-start(bf16[2,32,384]{2,1,0:T(8,128)(2,1)S(1)} %get-tuple-element.90), channel_id=1, source_target_pairs={{0,4},{2,6},{4,0},{6,2},{1,5},{3,7},{5,1},{7,3},{8,12},{10,14},{12... | collective-permute-start | bytes 147464 | tf_op jit(solution)/shard_map/ppermute | solution.py:286
  21.6 24.7 %collective-permute-start.7 = (bf16[1,128]{1,0:T(2,128)(2,1)S(1)}, bf16[1,128]{1,0:T(2,128)(2,1)S(1)}, u32[]{:S(2)}, u32[]{:S(2)}) collective-permute-start(bf16[1,128]{1,0:T(2,128)(2,1)S(1)} %reshape.229), channel_id=1, source_target_pairs={{0,1},{1,0},{2,3},{3,2},{4,5},{5,4},{6,7},{7,6},{8,9},{9,8},{10,11... | collective-permute-start | bytes 776 | tf_op jit(solution)/shard_map/ppermute | solution.py:286
  44.1 21.2 %collective-permute-start.19 = (bf16[4,2,32,384]{3,2,1,0:T(8,128)(2,1)}, bf16[4,2,32,384]{3,2,1,0:T(8,128)(2,1)}, u32[]{:S(2)}, u32[]{:S(2)}) collective-permute-start(bf16[4,2,32,384]{3,2,1,0:T(8,128)(2,1)} %get-tuple-element.86), channel_id=1, source_target_pairs={{0,16},{8,24},{16,0},{24,8},{1,17},{9,25},{17,1},{25,9},{2,18},{10... | collective-permute-start | bytes 589832 | tf_op jit(solution)/shard_map/ppermute | solution.py:286
  46.4 6.9 %collective-permute-start.10 = (bf16[2,128]{1,0:T(2,128)(2,1)S(1)}, bf16[2,128]{1,0:T(2,128)(2,1)S(1)}, u32[]{:S(2)}, u32[]{:S(2)}) collective-permute-start(bf16[2,128]{1,0:T(2,128)(2,1)S(1)} %pad_maximum_fusion.14), channel_id=1, source_target_pairs={{0,6},{2,4},{4,2},{6,0},{1,7},{3,5},{5,3},{7,1},{8,14},{10,12},{12... | collective-permute-start | bytes 1544 | tf_op jit(solution)/shard_map/ppermute | solution.py:286
  51.7 5.2 collective-permute-start.9
  51.7 5.2 collective-permute-start.8
  57.0 4.6 collective-permute-start.13
  57.8 5.3 %collective-permute-start.12 = (bf16[8,128]{1,0:T(8,128)(2,1)S(1)}, bf16[8,128]{1,0:T(8,128)(2,1)S(1)}, u32[]{:S(2)}, u32[]{:S(2)}) collective-permute-start(bf16[8,128]{1,0:T(8,128)(2,1)S(1)} %concatenate.68), channel_id=1, source_target_pairs={{0,16},{8,24},{16,0},{24,8},{1,17},{9,25},{17,1},{25,9},{2,18},{10... | collective-permute-start | bytes 6152 | tf_op jit(solution)/shard_map/ppermute | solution.py:286
  60.0 54.5 %collective-permute-start.3 = (bf16[256,1024]{1,0:T(8,128)(2,1)S(1)}, bf16[256,1024]{1,0:T(8,128)(2,1)S(1)}, u32[]{:S(2)}, u32[]{:S(2)}) collective-permute-start(bf16[256,1024]{1,0:T(8,128)(2,1)S(1)} %copy-done.2), channel_id=1, source_target_pairs={{0,4},{2,6},{4,0},{6,2},{1,5},{3,7},{5,1},{7,3},{8,12},{10,14},{12... | collective-permute-start | bytes 1572872 | tf_op jit(solution)/shard_map/ppermute | solution.py:286
  63.1 11.2 %collective-permute-start.18 = (bf16[4,2,32,384]{3,2,1,0:T(8,128)(2,1)}, bf16[4,2,32,384]{3,2,1,0:T(8,128)(2,1)S(1)}, u32[]{:S(2)}, u32[]{:S(2)}) collective-permute-start(bf16[4,2,32,384]{3,2,1,0:T(8,128)(2,1)} %get-tuple-element.86), channel_id=1, source_target_pairs={{0,8},{8,0},{16,24},{24,16},{1,9},{9,1},{17,25},{25,17},{2,10},{10... | collective-permute-start | bytes 589832 | tf_op jit(solution)/shard_map/ppermute | solution.py:286
  65.2 53.9 %collective-permute-start = (bf16[256,1024]{1,0:T(8,128)(2,1)S(1)}, bf16[256,1024]{1,0:T(8,128)(2,1)S(1)}, u32[]{:S(2)}, u32[]{:S(2)}) collective-permute-start(bf16[256,1024]{1,0:T(8,128)(2,1)S(1)} %copy-done.2), channel_id=1, source_target_pairs={{0,1},{1,0},{2,3},{3,2},{4,5},{5,4},{6,7},{7,6},{8,9},{9,8},{10,11... | collective-permute-start | bytes 1572872 | tf_op jit(solution)/shard_map/ppermute | solution.py:286
  65.2 53.4 %collective-permute-start.5 = (bf16[256,1024]{1,0:T(8,128)(2,1)S(1)}, bf16[256,1024]{1,0:T(8,128)(2,1)S(1)}, u32[]{:S(2)}, u32[]{:S(2)}) collective-permute-start(bf16[256,1024]{1,0:T(8,128)(2,1)S(1)} %copy-done.2), channel_id=1, source_target_pairs={{0,6},{2,4},{4,2},{6,0},{1,7},{3,5},{5,3},{7,1},{8,14},{10,12},{12... | collective-permute-start | bytes 1572872 | tf_op jit(solution)/shard_map/ppermute | solution.py:286
  74.2 40.2 %collective-permute-start.20 = (bf16[4,2,32,384]{3,2,1,0:T(8,128)(2,1)}, bf16[4,2,32,384]{3,2,1,0:T(8,128)(2,1)}, u32[]{:S(2)}, u32[]{:S(2)}) collective-permute-start(bf16[4,2,32,384]{3,2,1,0:T(8,128)(2,1)} %get-tuple-element.86), channel_id=1, source_target_pairs={{0,24},{8,16},{16,8},{24,0},{1,25},{9,17},{17,9},{25,1},{2,26},{10... | collective-permute-start | bytes 589832 | tf_op jit(solution)/shard_map/ppermute | solution.py:286
  74.9 46.0 %collective-permute-start.2 = (bf16[256,1024]{1,0:T(8,128)(2,1)S(1)}, bf16[256,1024]{1,0:T(8,128)(2,1)S(1)}, u32[]{:S(2)}, u32[]{:S(2)}) collective-permute-start(bf16[256,1024]{1,0:T(8,128)(2,1)S(1)} %collective-permute-done.1), channel_id=1, source_target_pairs={{0,1},{1,0},{2,3},{3,2},{4,5},{5,4},{6,7},{7,6},{8,9},{9,8},{10,11... | collective-permute-start | bytes 1572872 | tf_op jit(solution)/shard_map/ppermute | solution.py:286
  114.4 8.2 %collective-permute-start.4 = (bf16[256,1024]{1,0:T(8,128)(2,1)S(1)}, bf16[256,1024]{1,0:T(8,128)(2,1)S(1)}, u32[]{:S(2)}, u32[]{:S(2)}) collective-permute-start(bf16[256,1024]{1,0:T(8,128)(2,1)S(1)} %collective-permute-done.3), channel_id=1, source_target_pairs={{0,1},{1,0},{2,3},{3,2},{4,5},{5,4},{6,7},{7,6},{8,9},{9,8},{10,11... | collective-permute-start | bytes 1572872 | tf_op jit(solution)/shard_map/ppermute | solution.py:286
  118.6 5.6 %collective-permute-start.6 = (bf16[256,1024]{1,0:T(8,128)(2,1)S(1)}, bf16[256,1024]{1,0:T(8,128)(2,1)S(1)}, u32[]{:S(2)}, u32[]{:S(2)}) collective-permute-start(bf16[256,1024]{1,0:T(8,128)(2,1)S(1)} %collective-permute-done.5), channel_id=1, source_target_pairs={{0,1},{1,0},{2,3},{3,2},{4,5},{5,4},{6,7},{7,6},{8,9},{9,8},{10,11... | collective-permute-start | bytes 1572872 | tf_op jit(solution)/shard_map/ppermute | solution.py:286
  156.5 21.1 %collective-permute-start.23 = (bf16[512,128]{1,0:T(8,128)(2,1)S(1)}, bf16[512,128]{1,0:T(8,128)(2,1)S(1)}, u32[]{:S(2)}, u32[]{:S(2)}) collective-permute-start(bf16[512,128]{1,0:T(8,128)(2,1)S(1)} %get-tuple-element.77), channel_id=1, source_target_pairs={{0,6},{2,4},{4,2},{6,0},{1,7},{3,5},{5,3},{7,1},{8,14},{10,12},{12... | collective-permute-start | bytes 393224 | tf_op jit(solution)/shard_map/ppermute | solution.py:286
  157.7 29.5 %collective-permute-start.22 = (bf16[512,128]{1,0:T(8,128)(2,1)S(1)}, bf16[512,128]{1,0:T(8,128)(2,1)S(1)}, u32[]{:S(2)}, u32[]{:S(2)}) collective-permute-start(bf16[512,128]{1,0:T(8,128)(2,1)S(1)} %get-tuple-element.78), channel_id=1, source_target_pairs={{0,4},{2,6},{4,0},{6,2},{1,5},{3,7},{5,1},{7,3},{8,12},{10,14},{12... | collective-permute-start | bytes 393224 | tf_op jit(solution)/shard_map/ppermute | solution.py:286
  177.6 9.6 %collective-permute-start.21 = (bf16[512,128]{1,0:T(8,128)(2,1)S(1)}, bf16[512,128]{1,0:T(8,128)(2,1)S(1)}, u32[]{:S(2)}, u32[]{:S(2)}) collective-permute-start(bf16[512,128]{1,0:T(8,128)(2,1)S(1)} %get-tuple-element.79), channel_id=1, source_target_pairs={{0,2},{2,0},{4,6},{6,4},{1,3},{3,1},{5,7},{7,5},{8,10},{10,8},{12,... | collective-permute-start | bytes 393224 | tf_op jit(solution)/shard_map/ppermute | solution.py:286
  187.3 13.6 %collective-permute-start.26 = (bf16[256,1024]{1,0:T(8,128)(2,1)S(1)}, bf16[256,1024]{1,0:T(8,128)(2,1)}, u32[]{:S(2)}, u32[]{:S(2)}) collective-permute-start(bf16[256,1024]{1,0:T(8,128)(2,1)S(1)} %copy-done.18), channel_id=1, source_target_pairs={{0,1},{1,0},{2,3},{3,2},{4,5},{5,4},{6,7},{7,6},{8,9},{9,8},{10,11... | collective-permute-start | bytes 1572872 | tf_op jit(solution)/shard_map/ppermute | solution.py:286
  227.6 6.6 %collective-permute-start.29 = (bf16[256,1024]{1,0:T(8,128)(2,1)S(1)}, bf16[256,1024]{1,0:T(8,128)(2,1)S(1)}, u32[]{:S(2)}, u32[]{:S(2)}) collective-permute-start(bf16[256,1024]{1,0:T(8,128)(2,1)S(1)} %get-tuple-element.49), channel_id=1, source_target_pairs={{0,1},{1,0},{2,3},{3,2},{4,5},{5,4},{6,7},{7,6},{8,9},{9,8},{10,11... | collective-permute-start | bytes 1572872 | tf_op jit(solution)/shard_map/ppermute | solution.py:286
  232.8 95.4 %collective-permute-start.50 = (bf16[2,4,128,1024]{3,2,1,0:T(8,128)(2,1)}, bf16[2,4,128,1024]{3,2,1,0:T(8,128)(2,1)S(1)}, u32[]{:S(2)}, u32[]{:S(2)}) collective-permute-start(bf16[2,4,128,1024]{3,2,1,0:T(8,128)(2,1)} %dynamic-slice_bitcast_fusion), channel_id=1, source_target_pairs={{0,8},{8,0},{1,9},{9,1},{2,10},{10,2},{3,11},{11,3},{4,12},{12,4},... | collective-permute-start | bytes 6291464 | tf_op jit(solution)/shard_map/ppermute | solution.py:286
  235.9 8.9 %collective-permute-start.32 = (bf16[512,128]{1,0:T(8,128)(2,1)S(1)}, bf16[512,128]{1,0:T(8,128)(2,1)S(1)}, u32[]{:S(2)}, u32[]{:S(2)}) collective-permute-start(bf16[512,128]{1,0:T(8,128)(2,1)S(1)} %get-tuple-element.70), channel_id=1, source_target_pairs={{0,6},{2,4},{4,2},{6,0},{1,7},{3,5},{5,3},{7,1},{8,14},{10,12},{12... | collective-permute-start | bytes 393224 | tf_op jit(solution)/shard_map/ppermute | solution.py:286
  237.2 11.7 %collective-permute-start.31 = (bf16[512,128]{1,0:T(8,128)(2,1)S(1)}, bf16[512,128]{1,0:T(8,128)(2,1)S(1)}, u32[]{:S(2)}, u32[]{:S(2)}) collective-permute-start(bf16[512,128]{1,0:T(8,128)(2,1)S(1)} %get-tuple-element.71), channel_id=1, source_target_pairs={{0,4},{2,6},{4,0},{6,2},{1,5},{3,7},{5,1},{7,3},{8,12},{10,14},{12... | collective-permute-start | bytes 393224 | tf_op jit(solution)/shard_map/ppermute | solution.py:286
  237.2 11.7 %collective-permute-start.30 = (bf16[512,128]{1,0:T(8,128)(2,1)S(1)}, bf16[512,128]{1,0:T(8,128)(2,1)S(1)}, u32[]{:S(2)}, u32[]{:S(2)}) collective-permute-start(bf16[512,128]{1,0:T(8,128)(2,1)S(1)} %get-tuple-element.72), channel_id=1, source_target_pairs={{0,2},{2,0},{4,6},{6,4},{1,3},{3,1},{5,7},{7,5},{8,10},{10,8},{12,... | collective-permute-start | bytes 393224 | tf_op jit(solution)/shard_map/ppermute | solution.py:286
  297.9 8.8 %collective-permute-start.37 = (bf16[272,384]{1,0:T(8,128)(2,1)}, bf16[272,384]{1,0:T(8,128)(2,1)S(1)}, u32[]{:S(2)}, u32[]{:S(2)}) collective-permute-start(bf16[272,384]{1,0:T(8,128)(2,1)} %get-tuple-element.64), channel_id=1, source_target_pairs={{0,8},{8,0},{16,24},{24,16},{1,9},{9,1},{17,25},{25,17},{2,10},{10... | collective-permute-start | bytes 626696 | tf_op jit(solution)/shard_map/ppermute | solution.py:286
  298.3 12.4 %collective-permute-start.39 = (bf16[272,384]{1,0:T(8,128)(2,1)}, bf16[272,384]{1,0:T(8,128)(2,1)}, u32[]{:S(2)}, u32[]{:S(2)}) collective-permute-start(bf16[272,384]{1,0:T(8,128)(2,1)} %get-tuple-element.65), channel_id=1, source_target_pairs={{0,24},{8,16},{16,8},{24,0},{1,25},{9,17},{17,9},{25,1},{2,26},{10... | collective-permute-start | bytes 626696 | tf_op jit(solution)/shard_map/ppermute | solution.py:286
  300.8 11.1 %collective-permute-start.38 = (bf16[272,384]{1,0:T(8,128)(2,1)S(1)}, bf16[272,384]{1,0:T(8,128)(2,1)}, u32[]{:S(2)}, u32[]{:S(2)}) collective-permute-start(bf16[272,384]{1,0:T(8,128)(2,1)S(1)} %get-tuple-element.66), channel_id=1, source_target_pairs={{0,16},{8,24},{16,0},{24,8},{1,17},{9,25},{17,1},{25,9},{2,18},{10... | collective-permute-start | bytes 626696 | tf_op jit(solution)/shard_map/ppermute | solution.py:286
  316.5 8.4 %collective-permute-start.40 = (bf16[80,384]{1,0:T(8,128)(2,1)S(1)}, bf16[80,384]{1,0:T(8,128)(2,1)S(1)}, u32[]{:S(2)}, u32[]{:S(2)}) collective-permute-start(bf16[80,384]{1,0:T(8,128)(2,1)S(1)} %get-tuple-element.80), channel_id=1, source_target_pairs={{0,2},{2,0},{4,6},{6,4},{1,3},{3,1},{5,7},{7,5},{8,10},{10,8},{12,... | collective-permute-start | bytes 184328 | tf_op jit(solution)/shard_map/ppermute | solution.py:286
  316.5 8.3 %collective-permute-start.41 = (bf16[80,384]{1,0:T(8,128)(2,1)S(1)}, bf16[80,384]{1,0:T(8,128)(2,1)S(1)}, u32[]{:S(2)}, u32[]{:S(2)}) collective-permute-start(bf16[80,384]{1,0:T(8,128)(2,1)S(1)} %get-tuple-element.81), channel_id=1, source_target_pairs={{0,4},{2,6},{4,0},{6,2},{1,5},{3,7},{5,1},{7,3},{8,12},{10,14},{12... | collective-permute-start | bytes 184328 | tf_op jit(solution)/shard_map/ppermute | solution.py:286
  318.6 6.3 %collective-permute-start.42 = (bf16[80,384]{1,0:T(8,128)(2,1)S(1)}, bf16[80,384]{1,0:T(8,128)(2,1)S(1)}, u32[]{:S(2)}, u32[]{:S(2)}) collective-permute-start(bf16[80,384]{1,0:T(8,128)(2,1)S(1)} %get-tuple-element.82), channel_id=1, source_target_pairs={{0,6},{2,4},{4,2},{6,0},{1,7},{3,5},{5,3},{7,1},{8,14},{10,12},{12... | collective-permute-start | bytes 184328 | tf_op jit(solution)/shard_map/ppermute | solution.py:286
  324.2 83.5 %collective-permute-start.44 = (bf16[2,4,64,2560]{3,2,1,0:T(8,128)(2,1)}, bf16[2,4,64,2560]{3,2,1,0:T(8,128)(2,1)}, u32[]{:S(2)}, u32[]{:S(2)}) collective-permute-start(bf16[2,4,64,2560]{3,2,1,0:T(8,128)(2,1)} %fusion.12), channel_id=1, source_target_pairs={{0,16},{16,0},{1,17},{17,1},{2,18},{18,2},{3,19},{19,3},{4,20},{20... | collective-permute-start | bytes 7864328 | tf_op jit(solution)/shard_map/ppermute | solution.py:286
  331.0 71.9 %collective-permute-start.51 = (bf16[4,128,1024]{2,1,0:T(8,128)(2,1)S(1)}, bf16[4,128,1024]{2,1,0:T(8,128)(2,1)S(1)}, u32[]{:S(2)}, u32[]{:S(2)}) collective-permute-start(bf16[4,128,1024]{2,1,0:T(8,128)(2,1)S(1)} %dynamic-slice_bitcast_fusion.2), channel_id=1, source_target_pairs={{0,16},{16,0},{1,17},{17,1},{2,18},{18,2},{3,19},{19,3},{4,20},{20... | collective-permute-start | bytes 3145736 | tf_op jit(solution)/shard_map/ppermute | solution.py:286
  336.4 92.9 %collective-permute-start.33 = (bf16[4,256,1024]{2,1,0:T(8,128)(2,1)}, bf16[4,256,1024]{2,1,0:T(8,128)(2,1)}, u32[]{:S(2)}, u32[]{:S(2)}) collective-permute-start(bf16[4,256,1024]{2,1,0:T(8,128)(2,1)} %fusion.16), channel_id=1, source_target_pairs={{0,1},{1,0},{2,3},{3,2},{4,5},{5,4},{6,7},{7,6},{8,9},{9,8},{10,11... | collective-permute-start | bytes 6291464 | tf_op jit(solution)/shard_map/ppermute | solution.py:286
  404.3 14.7 %collective-permute-start.52 = (bf16[128,1024]{1,0:T(8,128)(2,1)}, bf16[128,1024]{1,0:T(8,128)(2,1)}, u32[]{:S(2)}, u32[]{:S(2)}) collective-permute-start(bf16[128,1024]{1,0:T(8,128)(2,1)} %get-tuple-element.60), channel_id=1, source_target_pairs={{0,2},{2,0},{4,6},{6,4},{1,3},{3,1},{5,7},{7,5},{8,10},{10,8},{12,... | collective-permute-start | bytes 786440 | tf_op jit(solution)/shard_map/ppermute | solution.py:286
  404.3 14.7 %collective-permute-start.54 = (bf16[128,1024]{1,0:T(8,128)(2,1)}, bf16[128,1024]{1,0:T(8,128)(2,1)}, u32[]{:S(2)}, u32[]{:S(2)}) collective-permute-start(bf16[128,1024]{1,0:T(8,128)(2,1)} %get-tuple-element.61), channel_id=1, source_target_pairs={{0,6},{2,4},{4,2},{6,0},{1,7},{3,5},{5,3},{7,1},{8,14},{10,12},{12... | collective-permute-start | bytes 786440 | tf_op jit(solution)/shard_map/ppermute | solution.py:286
  405.8 21.2 %collective-permute-start.53 = (bf16[128,1024]{1,0:T(8,128)(2,1)S(1)}, bf16[128,1024]{1,0:T(8,128)(2,1)}, u32[]{:S(2)}, u32[]{:S(2)}) collective-permute-start(bf16[128,1024]{1,0:T(8,128)(2,1)S(1)} %get-tuple-element.62), channel_id=1, source_target_pairs={{0,4},{2,6},{4,0},{6,2},{1,5},{3,7},{5,1},{7,3},{8,12},{10,14},{12... | collective-permute-start | bytes 786440 | tf_op jit(solution)/shard_map/ppermute | solution.py:286
  411.5 26.4 %collective-permute-start.45 = (bf16[4,64,2560]{2,1,0:T(8,128)(2,1)}, bf16[4,64,2560]{2,1,0:T(8,128)(2,1)}, u32[]{:S(2)}, u32[]{:S(2)}) collective-permute-start(bf16[4,64,2560]{2,1,0:T(8,128)(2,1)} %dynamic-slice_bitcast_fusion.1), channel_id=1, source_target_pairs={{0,8},{8,0},{1,9},{9,1},{2,10},{10,2},{3,11},{11,3},{4,12},{12,4},... | collective-permute-start | bytes 3932168 | tf_op jit(solution)/shard_map/ppermute | solution.py:286
  433.0 27.3 %collective-permute-start.34 = (bf16[256,1024]{1,0:T(8,128)(2,1)S(1)}, bf16[256,1024]{1,0:T(8,128)(2,1)S(1)}, u32[]{:S(2)}, u32[]{:S(2)}) collective-permute-start(bf16[256,1024]{1,0:T(8,128)(2,1)S(1)} %get-tuple-element.52), channel_id=1, source_target_pairs={{0,2},{2,0},{4,6},{6,4},{1,3},{3,1},{5,7},{7,5},{8,10},{10,8},{12,... | collective-permute-start | bytes 1572872 | tf_op jit(solution)/shard_map/ppermute | solution.py:286
  433.1 27.4 %collective-permute-start.36 = (bf16[256,1024]{1,0:T(8,128)(2,1)S(1)}, bf16[256,1024]{1,0:T(8,128)(2,1)S(1)}, u32[]{:S(2)}, u32[]{:S(2)}) collective-permute-start(bf16[256,1024]{1,0:T(8,128)(2,1)S(1)} %get-tuple-element.53), channel_id=1, source_target_pairs={{0,6},{2,4},{4,2},{6,0},{1,7},{3,5},{5,3},{7,1},{8,14},{10,12},{12... | collective-permute-start | bytes 1572872 | tf_op jit(solution)/shard_map/ppermute | solution.py:286
  434.8 62.4 %collective-permute-start.35 = (bf16[256,1024]{1,0:T(8,128)(2,1)S(1)}, bf16[256,1024]{1,0:T(8,128)(2,1)S(1)}, u32[]{:S(2)}, u32[]{:S(2)}) collective-permute-start(bf16[256,1024]{1,0:T(8,128)(2,1)S(1)} %get-tuple-element.54), channel_id=1, source_target_pairs={{0,4},{2,6},{4,0},{6,2},{1,5},{3,7},{5,1},{7,3},{8,12},{10,14},{12... | collective-permute-start | bytes 1572872 | tf_op jit(solution)/shard_map/ppermute | solution.py:286
  439.6 58.1 %collective-permute-start.46 = (bf16[64,2560]{1,0:T(8,128)(2,1)S(1)}, bf16[64,2560]{1,0:T(8,128)(2,1)S(1)}, u32[]{:S(2)}, u32[]{:S(2)}) collective-permute-start(bf16[64,2560]{1,0:T(8,128)(2,1)S(1)} %get-tuple-element.57), channel_id=1, source_target_pairs={{0,2},{2,0},{4,6},{6,4},{1,3},{3,1},{5,7},{7,5},{8,10},{10,8},{12,... | collective-permute-start | bytes 983048 | tf_op jit(solution)/shard_map/ppermute | solution.py:286
  440.8 56.9 %collective-permute-start.48 = (bf16[64,2560]{1,0:T(8,128)(2,1)S(1)}, bf16[64,2560]{1,0:T(8,128)(2,1)S(1)}, u32[]{:S(2)}, u32[]{:S(2)}) collective-permute-start(bf16[64,2560]{1,0:T(8,128)(2,1)S(1)} %get-tuple-element.58), channel_id=1, source_target_pairs={{0,6},{2,4},{4,2},{6,0},{1,7},{3,5},{5,3},{7,1},{8,14},{10,12},{12... | collective-permute-start | bytes 983048 | tf_op jit(solution)/shard_map/ppermute | solution.py:286
  460.4 47.1 %collective-permute-start.47 = (bf16[64,2560]{1,0:T(8,128)(2,1)S(1)}, bf16[64,2560]{1,0:T(8,128)(2,1)S(1)}, u32[]{:S(2)}, u32[]{:S(2)}) collective-permute-start(bf16[64,2560]{1,0:T(8,128)(2,1)S(1)} %get-tuple-element.59), channel_id=1, source_target_pairs={{0,4},{2,6},{4,0},{6,2},{1,5},{3,7},{5,1},{7,3},{8,12},{10,14},{12... | collective-permute-start | bytes 983048 | tf_op jit(solution)/shard_map/ppermute | solution.py:286
  (43 other events, 381.5 us)
Sparse Core Ops, SparseCore 0:
  11.0 170.6 all-gather.2
